TPU v7x, 128 devices: a whole 4x4x4 slice. The times are simulated.
128 devices in a mesh: dp: 8 (over x_hi, z), mp: 16 (over x_lo, y, core).
Axes of the slice: x: 4 (x_hi: 2, x_lo: 2; x = x_hi * 2 + x_lo), y: 4, z: 4, core: 2. Of those that a mesh axis runs over, the one named last changes fastest.
Arguments:
- tokens: bfloat16 [4096, 6144], P('dp'), may hold values from -6 to 6, as said below
- norm_gain: float32 [6144], replicated, may hold values from 0.5 to 1.5
- qkv_weight: bfloat16 [6144, 3, 4096], P('dp', None, 'mp'), as said below
- qk_gains: float32 [2, 128], replicated, may hold values from 0.6 to 6, as said below
- in_weight: bfloat16 [6144, 12288], P('dp', 'mp'), may hold values from -0.078125 to 0.078125
- in_bias: float32 [12288], P('mp'), may hold values from -3 to 3
- out_weight: bfloat16 [4096, 6144], P('mp', 'dp'), may hold values from -0.09375 to 0.09375
- mlp_out_weight: bfloat16 [12288, 6144], P('mp', 'dp'), may hold values from -0.0546875 to 0.0546875
- out_bias: float32 [6144], replicated, may hold values from -3 to 3
- targets: bfloat16 [4096, 3072], P('dp'), may hold values from -6 to 6
Outputs:
- gram_matrix: float32 [6144, 6144], P('mp', 'dp')
- cross_matrix: float32 [6144, 3072], P('mp', 'dp')
Inputs may be any that keep to these rules, and one draw needn't show every extreme that they name: `tokens`: activations of order one. `qkv_weight`: entries of order one over the square root of 6144. `qk_gains`: positive gains.
All inputs are finite; a program needn't handle non-finite values.
Results may differ from a plain program's by a relative error of at most 0.025.
Values may be sent and summed in bfloat16 or wider, within the bound.
No kernel may reach another device: no remote copies, remote signals or barrier semaphores. Data moves between devices by JAX's collectives and lax.ppermute only.
A program may use at most 128 MiB of HBM per device.

v0:
```python
import jax
import jax.numpy as jnp
from jax import lax
from jax.sharding import PartitionSpec as P

HEAD = 128


def layer_norm(inputs, norm_scale):
    center = jnp.mean(inputs, axis=-1, keepdims=True)
    spread = jnp.mean(jnp.square(inputs - center), axis=-1, keepdims=True)
    return (inputs - center) * lax.rsqrt(spread + 1e-06) * norm_scale


def on_device(
    tokens,
    norm_gain,
    qkv_weight,
    qk_gains,
    in_weight,
    in_bias,
    out_weight,
    mlp_out_weight,
    out_bias,
    targets,
):
    tok_rows = tokens.shape[0]
    feat_width = tokens.shape[1]
    token_values = tokens.astype(jnp.float32)
    normed = layer_norm(token_values, norm_gain).astype(jnp.bfloat16)
    qkv_width = qkv_weight.shape[1] * qkv_weight.shape[2]
    pieces = (
        lax.all_gather(qkv_weight, "dp", axis=0, tiled=True),
        lax.all_gather(in_weight, "dp", axis=0, tiled=True),
    )
    piece_rows = pieces[1].shape[0]
    qkv_piece = pieces[0].reshape(piece_rows, qkv_width)
    query_key_value = jnp.dot(normed, qkv_piece, preferred_element_type=jnp.float32)
    mlp_input = jnp.dot(normed, pieces[1], preferred_element_type=jnp.float32)
    head_count = qkv_weight.shape[2] // HEAD
    query_key_value = query_key_value.reshape(tok_rows, 3, head_count, HEAD)
    queries = layer_norm(query_key_value[:, 0], qk_gains[0]).astype(jnp.bfloat16)
    own_keys = layer_norm(query_key_value[:, 1], qk_gains[1]).astype(jnp.bfloat16)
    own_values = query_key_value[:, 2].astype(jnp.bfloat16)
    all_keys, all_values = (
        lax.all_gather(own_keys, "dp", axis=0, tiled=True),
        lax.all_gather(own_values, "dp", axis=0, tiled=True),
    )
    scores = jnp.einsum(
        "qhd,khd->hqk", queries, all_keys, preferred_element_type=jnp.float32
    ) * HEAD ** (-0.5)
    soft_weights = jax.nn.softmax(scores, axis=-1).astype(jnp.bfloat16)
    attended = jnp.einsum(
        "hqk,khd->qhd", soft_weights, all_values, preferred_element_type=jnp.float32
    )
    attended = attended.astype(jnp.bfloat16).reshape(tok_rows, head_count * HEAD)
    hidden = jax.nn.gelu(mlp_input + in_bias, approximate=False).astype(jnp.bfloat16)
    pieces = lax.all_gather((out_weight, mlp_out_weight), "dp", axis=1, tiled=True)
    branches = jnp.dot(attended, pieces[0], preferred_element_type=jnp.float32) + jnp.dot(
        hidden, pieces[1], preferred_element_type=jnp.float32
    )
    mp_index = lax.axis_index("mp")
    block_width = feat_width // lax.axis_size("mp")
    summed = lax.psum(branches.astype(jnp.bfloat16), "mp").astype(jnp.float32)
    block_output = (token_values + out_bias + summed).astype(jnp.bfloat16)
    own_block = lax.dynamic_slice_in_dim(block_output, mp_index * block_width, block_width, 1)
    total_tokens = tok_rows * lax.axis_size("dp")
    gram_part = (
        jnp.einsum("ti,tj->ij", own_block, block_output, preferred_element_type=jnp.float32)
        / total_tokens
    )
    cross_part = (
        jnp.einsum("ti,tj->ij", own_block, targets, preferred_element_type=jnp.float32)
        / total_tokens
    )
    gram_matrix, cross_matrix = (
        lax.psum_scatter(
            gram_part.astype(jnp.bfloat16), "dp", scatter_dimension=1, tiled=True
        ).astype(jnp.float32),
        lax.psum_scatter(
            cross_part.astype(jnp.bfloat16), "dp", scatter_dimension=1, tiled=True
        ).astype(jnp.float32),
    )
    return (gram_matrix, cross_matrix)


def solution(mesh):
    placed = (
        P("dp", None),
        P(),
        P("dp", None, "mp"),
        P(),
        P("dp", "mp"),
        P("mp"),
        P("mp", "dp"),
        P("mp", "dp"),
        P(),
        P("dp", None),
    )
    return jax.shard_map(
        on_device,
        mesh=mesh,
        in_specs=placed,
        out_specs=(P("mp", "dp"), P("mp", "dp")),
        check_vma=False,
    )
```

profile of v0, /device:TPU:1, one launch (start us, length us, event | category | flops | bytes accessed | tf_op | source)
XLA Modules:
  0.0 874.1 jit_solution(4574941792494428864)
XLA Ops:
  7.2 0.0 all-gather.8.cloned.1.call-start
  7.2 2.5 copy.17
  9.8 0.0 all-gather.8.cloned.1.call-update
  9.8 0.0 all-gather.14.cloned.1.call-start
  9.8 0.7 all-gather.14.cloned.1.call-update
  10.5 0.0 all-gather.16.cloned.1.call-start
  10.6 0.7 all-gather.16.cloned.1.call-update
  11.3 0.0 all-gather.10.cloned.1.call-start
  11.3 3.8 convert_reduce_fusion
  15.2 0.7 copy-done.1
  15.9 1.8 fusion.6
  17.7 112.3 %all-gather.8.cloned.1.call-done = bf16[6144,3,256]{0,2,1:T(8,128)(2,1)} async-done(((bf16[768,3,256]{0,2,1:T(8,128)(2,1)}), bf16[6144,3,256]{0,2,1:T(8,128)(2,1)}) %all-gather.8.cloned.1.call-update) | async-done | bytes 9437200 | tf_op jit(solution)/shard_map/all_gather | solution.py:33
  130.0 9.8 %fusion.13 = f32[512,3,2,128]{0,3,2,1:T(8,128)S(1)} fusion(bf16[3,2,128,6144]{3,2,1,0:T(8,128)(2,1)} %bitcast.56, bf16[512,6144]{1,0:T(8,128)(2,1)} %param.10, f32[6144]{0:T(1024)S(1)} %copy-done.5, f32[512]{0:T(512)S(1)} %add_rsqrt_fusion.2, f32[512]{0:T(512)S(1)} %broadcast_multiply_fusion.2), kind=kOutput, calls=%fused_computation.19 | convolution fusion | flops 4847566848 | bytes 17330176 | tf_op jit(solution)/shard_map/dot_general | solution.py:38
  139.9 0.1 slice_reduce_fusion.1
  140.0 0.1 multiply_reduce_fusion.2
  140.1 0.8 copy-done.2
  141.0 0.8 multiply_convert_fusion.2
  141.8 0.0 all-gather.10.cloned.1.call-update
  141.8 0.0 all-gather.18.cloned.1.call-start
  141.9 1.8 slice.37
  143.7 0.0 all-gather.18.cloned.1.call-update
  143.7 0.0 all-gather.12.cloned.1.call-start
  143.7 0.5 all-gather.12.cloned.1.call-update
  144.3 0.2 all-reduce.2.cloned.1.call-start
  144.5 102.3 %all-gather.14.cloned.1.call-done = bf16[6144,768]{1,0:T(8,128)(2,1)} async-done(((bf16[768,768]{1,0:T(8,128)(2,1)}), bf16[6144,768]{1,0:T(8,128)(2,1)}) %all-gather.14.cloned.1.call-update) | async-done | bytes 9437200 | tf_op jit(solution)/shard_map/all_gather | solution.py:34
  246.8 116.4 %all-gather.16.cloned.1.call-done = bf16[768,6144]{1,0:T(8,128)(2,1)} async-done(((bf16[768,768]{1,0:T(8,128)(2,1)}), bf16[768,6144]{1,0:T(8,128)(2,1)}) %all-gather.16.cloned.1.call-update) | async-done | bytes 9437200 | tf_op jit(solution)/shard_map/all_gather | solution.py:58
  363.2 26.6 %fusion.31 = f32[512,6144]{1,0:T(8,128)} fusion(bf16[768,6144]{1,0:T(8,128)(2,1)} %all-gather.16.cloned.1.call-done, bf16[6144,768]{1,0:T(8,128)(2,1)} %all-gather.14.cloned.1.call-done, f32[768]{0:T(1024)S(1)} %copy-done.6, bf16[512,6144]{1,0:T(8,128)(2,1)} %param.10, f32[6144]{0:T(1024)S(1)} %copy-done.5, f32[512]{0:T(512)S(1)} %add_rsqrt_fusion.2, ...), kind=kOutput, calls=%fused_computation.44 | convolution fusion | flops 9705357312 | bytes 37780480 | tf_op jit(solution)/shard_map/dot_general | solution.py:59
  389.8 28.4 %all-gather.10.cloned.1.call-done = bf16[4096,2,128]{0,2,1:T(8,128)(2,1)} async-done(((bf16[512,2,128]{0,2,1:T(8,128)(2,1)}), bf16[4096,2,128]{0,2,1:T(8,128)(2,1)}) %all-gather.10.cloned.1.call-update) | async-done | bytes 2097168 | tf_op jit(solution)/shard_map/all_gather | solution.py:46
  418.2 10.6 %fusion.70 = (f32[2,512]{1,0:T(2,128)S(1)}, f32[2,512,4096]{2,1,0:T(8,128)}) fusion(bf16[4096,2,128]{0,2,1:T(8,128)(2,1)} %all-gather.10.cloned.1.call-done, f32[512,3,2,128]{0,3,2,1:T(8,128)} %copy-done.2, f32[128]{0:T(128)S(1)} %get-tuple-element.6, f32[512,2]{0,1:T(2,128)S(1)} %add_rsqrt_fusion.1, f32[512,2]{0,1:T(2,128)S(1)} %get-tuple-element.11), kind=kOutput, calls=%fused_computation.97 | convolution fusion | flops 1086853120 | bytes 19411456 | tf_op jit(solution)/shard_map/sub | solution.py:52
  428.8 44.4 %all-gather.18.cloned.1.call-done = bf16[4096,1,2,128]{0,3,2,1:T(8,128)(2,1)} async-done(((bf16[512,1,2,128]{0,3,2,1:T(8,128)(2,1)}), bf16[4096,1,2,128]{0,3,2,1:T(8,128)(2,1)}) %all-gather.18.cloned.1.call-update) | async-done | bytes 2097168 | tf_op jit(solution)/shard_map/all_gather | solution.py:47
  473.2 9.4 %fusion.28 = bf16[2,128,512]{2,1,0:T(8,128)(2,1)S(1)} fusion(f32[2,512,4096]{2,1,0:T(8,128)} %get-tuple-element.9, f32[2,512]{1,0:T(2,128)S(1)} %get-tuple-element.8, bf16[4096,1,2,128]{0,3,2,1:T(8,128)(2,1)} %all-gather.18.cloned.1.call-done), kind=kOutput, calls=%fused_computation.43 | convolution fusion | flops 1082261504 | bytes 19140608 | tf_op jit(solution)/shard_map/hqk,khd->qhd/dot_general | solution.py:53
  482.6 53.1 %all-gather.12.cloned.1.call-done = bf16[256,6144]{1,0:T(8,128)(2,1)} async-done(((bf16[256,768]{1,0:T(8,128)(2,1)}), bf16[256,6144]{1,0:T(8,128)(2,1)}) %all-gather.12.cloned.1.call-update) | async-done | bytes 3145744 | tf_op jit(solution)/shard_map/all_gather | solution.py:58
  535.7 10.0 %add_convert_fusion = bf16[512,6144]{1,0:T(8,128)(2,1)} fusion(f32[512,6144]{1,0:T(8,128)} %fusion.31, bf16[512,256]{0,1:T(8,128)(2,1)S(1)} %bitcast.54, bf16[256,6144]{1,0:T(8,128)(2,1)} %all-gather.12.cloned.1.call-done), kind=kOutput, calls=%fused_computation.15 | convolution fusion | flops 1616904192 | bytes 22282240 | tf_op jit(solution)/shard_map/dot_general | solution.py:59
  545.7 0.0 all-reduce.2.cloned.1.call-update
  545.7 0.0 reduce-scatter.7.cloned.1.call-start
  545.8 133.3 %all-reduce.2.cloned.1.call-done = bf16[512,6144]{1,0:T(8,128)(2,1)} async-done(((bf16[512,6144]{1,0:T(8,128)(2,1)}), bf16[512,6144]{1,0:T(8,128)(2,1)}) %all-reduce.2.cloned.1.call-update) | async-done | bytes 6291472 | tf_op jit(solution)/shard_map/psum | solution.py:64
  679.1 10.1 %fusion.10 = bf16[512,6144]{1,0:T(8,128)(2,1)} fusion(bf16[512,6144]{1,0:T(8,128)(2,1)} %param.10, bf16[512,6144]{1,0:T(8,128)(2,1)} %all-reduce.2.cloned.1.call-done, f32[6144]{0:T(1024)S(1)} %copy-done.3), kind=kLoop, calls=%fused_computation.14 | loop fusion | flops 15728640 | bytes 18898944 | tf_op jit(solution)/shard_map/convert_element_type | solution.py:65
  689.2 3.9 multiply_convert_fusion.1
  693.1 4.3 copy.23
  697.4 0.0 reduce-scatter.7.cloned.1.call-update
  697.5 0.0 reduce-scatter.5.cloned.1.call-start
  697.5 7.8 multiply_convert_fusion
  705.4 0.0 reduce-scatter.5.cloned.1.call-update
  705.4 69.5 %reduce-scatter.7.cloned.1.call-done = bf16[384,384]{1,0:T(8,128)(2,1)} async-done(((bf16[3072,384]{1,0:T(8,128)(2,1)}), bf16[384,384]{1,0:T(8,128)(2,1)}) %reduce-scatter.7.cloned.1.call-update) | async-done | bytes 294928
  774.9 1.2 copy.24
  776.0 0.9 convert_element_type.64
  776.9 88.5 %reduce-scatter.5.cloned.1.call-done = bf16[384,768]{1,0:T(8,128)(2,1)} async-done(((bf16[384,6144]{1,0:T(8,128)(2,1)}), bf16[384,768]{1,0:T(8,128)(2,1)}) %reduce-scatter.5.cloned.1.call-update) | async-done | bytes 589840 | tf_op jit(solution)/shard_map/reduce_scatter | solution.py:77
  865.4 2.2 convert_element_type.62
  (18 shorter events, 0.1 us)
Async XLA Ops:
  7.2 682.0 %copy-start = (bf16[512,3072]{1,0:T(8,128)(2,1)S(1)}, bf16[512,3072]{1,0:T(8,128)(2,1)}, u32[]{:S(2)}) copy-start(bf16[512,3072]{1,0:T(8,128)(2,1)} %param.19) | copy-start | bytes 9437188
  7.2 122.8 %all-gather.8.cloned.1.call-start = ((), (), s32[]{:S(2)}) async-start(), calls=%async_computation.2 | async-start | bytes 10616832 | tf_op jit(solution)/shard_map/all_gather | solution.py:33
  9.8 1.6 copy-start.4
  9.8 237.0 %all-gather.14.cloned.1.call-start = ((), (), s32[]{:S(2)}) async-start(), calls=%async_computation.5 | async-start | bytes 10616832 | tf_op jit(solution)/shard_map/all_gather | solution.py:34
  10.5 352.6 %all-gather.16.cloned.1.call-start = ((), (), s32[]{:S(2)}) async-start(), calls=%async_computation.6 | async-start | bytes 10616832 | tf_op jit(solution)/shard_map/all_gather | solution.py:58
  11.3 406.9 %all-gather.10.cloned.1.call-start = ((), (), s32[]{:S(2)}) async-start(), calls=%async_computation.3 | async-start | bytes 2359296 | tf_op jit(solution)/shard_map/all_gather | solution.py:46
  11.3 4.6 copy-start.1
  15.9 114.1 %copy-start.5 = (f32[6144]{0:T(1024)S(1)}, f32[6144]{0:T(1024)}, u32[]{:S(2)}) copy-start(f32[6144]{0:T(1024)} %param.11) | copy-start | bytes 73732
  139.8 1.1 copy-start.2
  139.9 223.3 %copy-start.6 = (f32[768]{0:T(1024)S(1)}, f32[768]{0:T(1024)}, u32[]{:S(2)}) copy-start(f32[768]{0:T(1024)} %param.15) | copy-start | bytes 9220
  141.8 331.4 %all-gather.18.cloned.1.call-start = ((), (), s32[]{:S(2)}) async-start(), calls=%async_computation.9 | async-start | bytes 2359296 | tf_op jit(solution)/shard_map/all_gather | solution.py:47
  143.7 392.0 %all-gather.12.cloned.1.call-start = ((), (), s32[]{:S(2)}) async-start(), calls=%async_computation.4 | async-start | bytes 3538944 | tf_op jit(solution)/shard_map/all_gather | solution.py:58
  144.3 534.8 %all-reduce.2.cloned.1.call-start = ((), (), s32[]{:S(2)}) async-start(), calls=%async_computation.7 | async-start | bytes 12582912 | tf_op jit(solution)/shard_map/psum | solution.py:64
  545.7 133.4 %copy-start.3 = (f32[6144]{0:T(1024)S(1)}, f32[6144]{0:T(1024)}, u32[]{:S(2)}) copy-start(f32[6144]{0:T(1024)} %param.18) | copy-start | bytes 73732
  545.7 229.1 %reduce-scatter.7.cloned.1.call-start = ((), (), s32[]{:S(2)}) async-start(), calls=%async_computation.10 | async-start | bytes 2654208
  697.5 168.0 %reduce-scatter.5.cloned.1.call-start = ((), (), s32[]{:S(2)}) async-start(), calls=%async_computation.8 | async-start | bytes 5308416 | tf_op jit(solution)/shard_map/reduce_scatter | solution.py:77
Sparse Core Ops, SparseCore 0:
  10.9 119.0 all-gather.7
  132.3 114.4 all-gather.13
  249.2 113.9 all-gather.15
  365.8 52.3 all-gather.9
  420.8 52.3 all-gather.17
  475.4 60.2 all-gather.11
  545.8 133.1 all-reduce.1
  697.6 77.2 reduce-scatter.6
  778.8 86.5 reduce-scatter.4
where the time goes:
time: 875 us; the launch traced here: 874 us
  waiting for transfers between devices  750 us (86%)
  matrix products  78.2 us (9%)
  other arithmetic  19.8 us (2%)
  between operations  13.9 us (2%)
  local copies, waits for them, and re-layouts  11.4 us (1%)
    all_gather x2, waiting for transfers between devices, on_device(): lax.all_gather((out_weight, mlp_out_weight), 'dp', axis=1, tiled=True)  169 us
    psum x1, waiting for transfers between devices, on_device(): summed = lax.psum(branches.astype(jnp.bfloat16), 'mp').astype(jnp.float32)  133 us
    all_gather x1, waiting for transfers between devices, on_device(): lax.all_gather(qkv_weight, 'dp', axis=0, tiled=True)  112 us
    all_gather x1, waiting for transfers between devices, on_device(): lax.all_gather(in_weight, 'dp', axis=0, tiled=True)  102 us
    reduce_scatter x1, waiting for transfers between devices, on_device(): lax.psum_scatter(gram_part.astype(jnp.bfloat16), 'dp', scatter_dimension=...  88.5 us
    unnamed x10, waiting for transfers between devices  71.5 us
    all_gather x1, waiting for transfers between devices, on_device(): lax.all_gather(own_values, 'dp', axis=0, tiled=True)  44.4 us
    all_gather x1, waiting for transfers between devices, on_device(): lax.all_gather(own_keys, 'dp', axis=0, tiled=True)  28.4 us
  transfers between devices with their start and end apart: 9, of which 9 were waited for; matrix products, arithmetic and copies ran while one was open for 9% of the time, Pallas kernels for 0%

commit v1 on v0

v1 whole, which is shorter than its diff:
```python
import jax
import jax.numpy as jnp
from jax import lax
from jax.sharding import Mesh, PartitionSpec as P

HEAD = 128
BF = jnp.bfloat16
F32 = jnp.float32


def layer_norm(inputs, norm_scale):
    center = jnp.mean(inputs, axis=-1, keepdims=True)
    spread = jnp.mean(jnp.square(inputs - center), axis=-1, keepdims=True)
    return (inputs - center) * lax.rsqrt(spread + 1e-06) * norm_scale


def swap(x, axis, mask):
    size = lax.axis_size(axis)
    return lax.ppermute(x, axis, [(i, i ^ mask) for i in range(size)])


def shift(x, axis, step):
    size = lax.axis_size(axis)
    return lax.ppermute(x, axis, [(i, (i + step) % size) for i in range(size)])


def dyn(x, start, size, axis):
    return lax.dynamic_slice_in_dim(x, start, size, axis)


def dot(a, b):
    return jnp.dot(a, b, preferred_element_type=F32)


def ring_gather(x, axis):
    below = shift(x, axis, 1)
    above = shift(x, axis, -1)
    half = x.shape[0] // 2
    far = jnp.concatenate([shift(below[:half], axis, 1), shift(above[half:], axis, -1)])
    return [x, below, far, above]


def place(blocks, index, count, rows):
    out = jnp.zeros((count * rows,) + blocks[0].shape[1:], blocks[0].dtype)
    for distance, block in enumerate(blocks):
        at = lax.rem(index - distance + count, count)
        out = lax.dynamic_update_slice_in_dim(out, block, at * rows, 0)
    return out


def on_device(
    tokens,
    norm_gain,
    qkv_weight,
    qk_gains,
    in_weight,
    in_bias,
    out_weight,
    mlp_out_weight,
    out_bias,
    targets,
):
    xh, z, xl, y, c = (lax.axis_index(a) for a in ("xh", "z", "xl", "y", "c"))
    rows, width = tokens.shape
    half = width // 2
    block = width // 8
    target_block = targets.shape[1] // 8
    piece = rows // 16

    by_head = qkv_weight.reshape(block, 3, 2, HEAD)
    keep_qkv = dyn(by_head, xh, 1, 2).reshape(block, 3 * HEAD)
    give_qkv = dyn(by_head, 1 - xh, 1, 2).reshape(block, 3 * HEAD)
    hid = in_weight.shape[1] // 2
    keep_in = dyn(in_weight, xh * hid, hid, 1)
    give_in = dyn(in_weight, (1 - xh) * hid, hid, 1)
    got_qkv = swap(give_qkv, "xh", 1)
    qkv_own = lax.all_gather(keep_qkv, "z", axis=0, tiled=True)
    qkv_par = lax.all_gather(got_qkv, "z", axis=0, tiled=True)

    token_values = tokens.astype(F32)
    center = jnp.mean(token_values, axis=-1, keepdims=True)
    spread = jnp.mean(jnp.square(token_values - center), axis=-1, keepdims=True)
    scale = lax.rsqrt(spread + 1e-06)

    def normed_half(which):
        part = dyn(tokens, which * half, half, 1).astype(F32)
        gain = dyn(norm_gain, which * half, half, 0)
        return ((part - center) * scale * gain).astype(BF)

    norm_own, norm_par = normed_half(xh), normed_half(1 - xh)
    share = rows // 8

    def from_partner(x):
        mine = dyn(x, (y * 2 + c) * share, share, 0)
        got = swap(mine, "xh", 1)
        around = place(ring_gather(got, "y"), y, 4, share)
        other = swap(around, "c", 1)
        first = jnp.where(c == 0, around, other).reshape(4, 1, share, half)
        second = jnp.where(c == 0, other, around).reshape(4, 1, share, half)
        return jnp.concatenate([first, second], axis=1).reshape(rows, half)

    far_own, far_par = from_partner(norm_par), from_partner(norm_own)
    got_in = swap(give_in, "xh", 1)
    in_own = lax.all_gather(keep_in, "z", axis=0, tiled=True)
    in_par = lax.all_gather(got_in, "z", axis=0, tiled=True)

    left = jnp.concatenate([norm_own, far_own])
    right = jnp.concatenate([norm_par, far_par])
    qkv = dot(left, qkv_own) + dot(right, qkv_par)
    queries = layer_norm(qkv[:, :HEAD], qk_gains[0]).astype(BF)
    own_keys = layer_norm(qkv[:, HEAD : 2 * HEAD], qk_gains[1]).astype(BF)
    own_kv = jnp.concatenate([own_keys, qkv[:, 2 * HEAD :].astype(BF)], axis=1)
    all_kv = lax.all_gather(own_kv, "z", axis=0, tiled=True)

    bias = dyn(in_bias, xh * hid, hid, 0)
    mlp_input = dot(left, in_own) + dot(right, in_par)
    hidden = jax.nn.gelu(mlp_input + bias, approximate=False).astype(BF)

    far_out, far_mlp = swap(out_weight, "xh", 1), swap(mlp_out_weight, "xh", 1)

    def to_tokens(x):
        got = swap(x[rows:], "xh", 1)
        mine = x[:rows]
        mine = jnp.where(xh == 0, jnp.concatenate([mine, got], axis=1), jnp.concatenate([got, mine], axis=1))
        return lax.all_gather(mine, "z", axis=0, tiled=False)

    hidden = to_tokens(hidden)

    all_keys, all_values = all_kv[:, :HEAD], all_kv[:, HEAD:]
    scores = jnp.einsum("qd,kd->qk", queries, all_keys, preferred_element_type=F32) * HEAD ** (-0.5)
    soft_weights = jax.nn.softmax(scores, axis=-1).astype(BF)
    attended = dot(soft_weights, all_values).astype(BF)
    attended = to_tokens(attended)

    at = ((c * 4 + y) * 2 + xl) * piece
    own_rows = dyn(tokens, at, piece, 0).reshape(piece, 2, 4, block).transpose(2, 0, 1, 3)
    residual = lax.all_to_all(own_rows, "z", split_axis=0, concat_axis=0, tiled=True)
    own_targets = dyn(targets, at, piece, 0).reshape(piece, 8, target_block).transpose(1, 0, 2)
    own_targets = lax.all_to_all(own_targets, ("xh", "z"), split_axis=0, concat_axis=0, tiled=True)
    all_targets = lax.all_gather(own_targets, ("xl", "y", "c"), axis=0, tiled=True)

    part_rows = rows // 2

    def partial(start, out_w, mlp_w):
        a = dyn(attended, start, part_rows, 1).reshape(4 * part_rows, -1)
        h = dyn(hidden, start, part_rows, 1).reshape(4 * part_rows, -1)
        return (dot(a, out_w) + dot(h, mlp_w)).reshape(4, part_rows, block)

    def over_core(out_w, mlp_w):
        give = partial((1 - c) * part_rows, out_w, mlp_w).astype(BF)
        got = swap(give, "c", 1)
        return partial(c * part_rows, out_w, mlp_w) + got.astype(F32)

    quarter = part_rows // 4

    def over_y(x, first, second):
        def at_index(i):
            return dyn(x, i * quarter, quarter, 1)

        third = first ^ second
        one = swap(at_index(y ^ third).astype(BF), "y", first)
        two = swap(at_index(y ^ first).astype(BF), "y", first)
        far = at_index(y ^ second) + one.astype(F32)
        return at_index(y) + two.astype(F32) + swap(far.astype(BF), "y", second).astype(F32)

    def over_xl(x):
        got = swap(dyn(x, (1 - xl) * piece, piece, 1).astype(BF), "xl", 1)
        return dyn(x, xl * piece, piece, 1) + got.astype(F32)

    sum_own = over_xl(over_y(over_core(out_weight, mlp_out_weight), 1, 3))
    sum_par = over_xl(over_y(over_core(far_out, far_mlp), 3, 1))

    def finish(total, which):
        base = dyn(residual, which, 1, 2).reshape(4, piece, block).astype(F32)
        return (base + dyn(out_bias, (which * 4 + z) * block, block, 0) + total).astype(BF)

    mine = finish(sum_own, xh)
    theirs = swap(finish(sum_par, 1 - xh), "xh", 1)
    out_piece = jnp.where(xh == 0, jnp.concatenate([mine, theirs]), jnp.concatenate([theirs, mine]))
    out_piece = out_piece.reshape(8 * piece, block)

    columns = lax.all_gather(out_piece, ("xl", "y", "c"), axis=0, tiled=True)
    turned = lax.ppermute(
        out_piece,
        ("xh", "z", "xl", "y"),
        [(a * 8 + b, b * 8 + a) for a in range(8) for b in range(8)],
    )
    narrow = block // 2
    stay = dyn(turned, c * narrow, narrow, 1)
    come = swap(dyn(turned, (1 - c) * narrow, narrow, 1), "c", 1)
    pair = jnp.where(c == 0, jnp.concatenate([stay, come]), jnp.concatenate([come, stay]))
    own_columns = lax.all_gather(pair, ("xh", "z"), axis=0, tiled=True)

    total_tokens = rows * 8
    gram = jnp.einsum("ti,tj->ij", own_columns, columns, preferred_element_type=F32) / total_tokens
    all_targets = all_targets.reshape(total_tokens, target_block)
    cross = jnp.einsum("ti,tj->ij", own_columns, all_targets, preferred_element_type=F32) / total_tokens
    return gram, cross


def solution(mesh):
    fine = Mesh(mesh.devices.reshape(2, 4, 2, 4, 2), ("xh", "z", "xl", "y", "c"))
    dp, mp = ("xh", "z"), ("xl", "y", "c")
    placed = (
        P(dp, None),
        P(),
        P(dp, None, mp),
        P(),
        P(dp, mp),
        P(mp),
        P(mp, dp),
        P(mp, dp),
        P(),
        P(dp, None),
    )
    return jax.shard_map(
        on_device,
        mesh=fine,
        in_specs=placed,
        out_specs=(P(mp, dp), P(mp, dp)),
        check_vma=False,
    )
```

time: 875 us -> 511 us (0.58)
  waiting for transfers between devices: 750 us -> 264 us
  starting transfers between devices: 0.54 us -> 67.2 us
  local copies, waits for them, and re-layouts: 11.4 us -> 42.1 us
  other arithmetic: 19.8 us -> 39.7 us
    all_gather x6 -> x10, waiting for transfers between devices: 457 us -> 168 us  [the longest x1 79.3 us: on_device(): own_columns = lax.all_gather(pair, ('xh', 'z'), axis=0, tiled=True)]
    psum x1 -> x0, waiting for transfers between devices: 133 us -> none  [on_device(): summed = lax.psum(branches.astype(jnp.bfloat16), 'mp').astype(jnp.float32)]
    reduce_scatter x1 -> x0, waiting for transfers between devices: 88.5 us -> none  [on_device(): lax.psum_scatter(gram_part.astype(jnp.bfloat16), 'dp', scatter_dimension=...]
    ppermute x0 -> x31, waiting for transfers between devices: none -> 75.5 us  [the longest x22 63.4 us: swap(): return lax.ppermute(x, axis, [(i, i ^ mask) for i in range(size)])]
    unnamed x10, waiting for transfers between devices: 71.5 us -> 0.94 us
    ppermute x0 -> x31, starting transfers between devices: none -> 58.4 us  [the longest x22 47.8 us: swap(): return lax.ppermute(x, axis, [(i, i ^ mask) for i in range(size)])]
    all_to_all x0 -> x2, waiting for transfers between devices: none -> 19.3 us  [the longest x1 19.3 us: on_device(): lax.all_to_all(own_targets, ('xh', 'z'), split_axis=0, concat_axis=0, til...]
    reduce_sum x0 -> x3, other arithmetic: none -> 14.8 us  [the longest x1 9.15 us: on_device(): soft_weights = jax.nn.softmax(scores, axis=-1).astype(BF)]
  transfers between devices with their start and end apart: 9 -> 43, of which waited for: 9 -> 21; matrix products, arithmetic and copies ran while one was open for 9% -> 26% of each run, Pallas kernels for 0% -> 0%
where the time goes in v1:
time: 511 us; the launch traced here: 503 us
  waiting for transfers between devices  264 us (52%)
  matrix products  74.7 us (15%)
  starting transfers between devices  67.2 us (13%)
  local copies, waits for them, and re-layouts  42.1 us (8%)
  other arithmetic  39.7 us (8%)
  between operations  15 us (3%)
    all_gather x1, waiting for transfers between devices, on_device(): own_columns = lax.all_gather(pair, ('xh', 'z'), axis=0, tiled=True)  79.3 us
    ppermute x22, waiting for transfers between devices, swap(): return lax.ppermute(x, axis, [(i, i ^ mask) for i in range(size)])  63.4 us
    dot_general x13, matrix products, dot(): return jnp.dot(a, b, preferred_element_type=F32)  52.2 us
    ppermute x22, starting transfers between devices, swap(): return lax.ppermute(x, axis, [(i, i ^ mask) for i in range(size)])  47.8 us
    all_gather x1, waiting for transfers between devices, on_device(): columns = lax.all_gather(out_piece, ('xl', 'y', 'c'), axis=0, tiled=True)  37.5 us
    all_gather x1, waiting for transfers between devices, on_device(): in_own = lax.all_gather(keep_in, 'z', axis=0, tiled=True)  25.1 us
    all_to_all x1, waiting for transfers between devices, on_device(): lax.all_to_all(own_targets, ('xh', 'z'), split_axis=0, concat_axis=0, til...  19.3 us
    dynamic_slice x13, local copies, waits for them, and re-layouts, dyn(): return lax.dynamic_slice_in_dim(x, start, size, axis)  14.1 us
  transfers between devices with their start and end apart: 43, of which 21 were waited for; matrix products, arithmetic and copies ran while one was open for 26% of the time, Pallas kernels for 0%

profile of v1, /device:TPU:1, one launch (start us, length us, event | category | flops | bytes accessed | tf_op | source)
XLA Modules:
  0.0 502.9 jit_solution(12195864690773064870)
XLA Ops:
  7.2 2.5 copy.42
  11.9 3.6 collective-permute-start.12
  15.5 12.7 %collective-permute-done.12 = bf16[768,384]{0,1:T(8,128)(2,1)} collective-permute-done((bf16[768,384]{0,1:T(8,128)(2,1)S(1)}, bf16[768,384]{0,1:T(8,128)(2,1)}, u32[]{:S(2)}, u32[]{:S(2)}) %collective-permute-start.12) | collective-permute-done | bytes 589856 | tf_op jit(solution)/shard_map/ppermute | solution.py:19
  28.3 3.8 convert_reduce_fusion
  34.6 2.9 multiply_convert_fusion
  39.2 3.2 collective-permute-start.6
  44.1 6.0 %collective-permute-done.6 = bf16[64,3072]{1,0:T(8,128)(2,1)} collective-permute-done((bf16[64,3072]{1,0:T(8,128)(2,1)S(1)}, bf16[64,3072]{1,0:T(8,128)(2,1)}, u32[]{:S(2)}, u32[]{:S(2)}) %collective-permute-start.6) | collective-permute-done | bytes 393248 | tf_op jit(solution)/shard_map/ppermute | solution.py:19
  50.2 3.0 collective-permute-start.9
  53.2 5.4 %collective-permute-done = bf16[64,3072]{1,0:T(8,128)(2,1)} collective-permute-done((bf16[64,3072]{1,0:T(8,128)(2,1)}, bf16[64,3072]{1,0:T(8,128)(2,1)}, u32[]{:S(2)}, u32[]{:S(2)}) %collective-permute-start) | collective-permute-done | bytes 393248 | tf_op jit(solution)/shard_map/ppermute | solution.py:19
  69.1 4.3 collective-permute-done.10
  77.1 4.2 collective-permute-start.11
  86.9 4.3 collective-permute-done.4
  103.3 7.3 %fusion.5 = f32[1024,384]{0,1:T(8,128)} fusion(bf16[3072,384]{0,1:T(8,128)(2,1)} %all-gather.13.cloned.1.call-done, bf16[512,3072]{1,0:T(8,128)(2,1)} %bitcast.81, bf16[512,3072]{1,0:T(8,128)(2,1)} %copy-done.8), kind=kOutput, calls=%fused_computation.14 | convolution fusion | flops 2428502016 | bytes 10223616 | tf_op jit(solution)/shard_map/dot_general | solution.py:32
  110.6 6.6 %fusion.33 = f32[1024,384]{0,1:T(8,128)S(1)} fusion(f32[1024,384]{0,1:T(8,128)} %fusion.5, bf16[3072,384]{0,1:T(8,128)(2,1)} %all-gather.11.cloned.1.call-done, bf16[512,3072]{1,0:T(8,128)(2,1)} %bitcast.79, bf16[512,3072]{1,0:T(8,128)(2,1)} %copy-done.7), kind=kOutput, calls=%fused_computation.128 | convolution fusion | flops 2428895232 | bytes 11796480 | tf_op jit(solution)/shard_map/dot_general | solution.py:32
  121.4 2.8 collective-permute-start.14
  124.2 13.7 %collective-permute-done.14 = bf16[768,384]{1,0:T(8,128)(2,1)} collective-permute-done((bf16[768,384]{1,0:T(8,128)(2,1)S(1)}, bf16[768,384]{1,0:T(8,128)(2,1)}, u32[]{:S(2)}, u32[]{:S(2)}) %collective-permute-start.14) | collective-permute-done | bytes 589856 | tf_op jit(solution)/shard_map/ppermute | solution.py:19
  139.2 10.7 %all-gather.15.cloned.1.call-done = bf16[4096,256]{0,1:T(8,128)(2,1)} async-done(((bf16[1024,256]{0,1:T(8,128)(2,1)}), bf16[4096,256]{0,1:T(8,128)(2,1)}) %all-gather.15.cloned.1.call-update) | async-done | bytes 2097168 | tf_op jit(solution)/shard_map/all_gather | solution.py:113
  150.0 9.6 %multiply_reduce_fusion = (f32[1024]{0:T(1024)S(1)}, f32[1024,4096]{1,0:T(8,128)}) fusion(bf16[4096,256]{0,1:T(8,128)(2,1)} %all-gather.15.cloned.1.call-done, f32[1024,384]{0,1:T(8,128)} %copy-done.4, f32[128]{0:T(128)S(1)} %get-tuple-element.36, f32[1024]{0:T(1024)S(1)} %add_rsqrt_fusion.1, f32[1024]{0:T(1024)S(1)} %get-tuple-element.41), kind=kOutput, calls=%fused_computation.2 | convolution fusion | flops 1082653696 | bytes 18362880 | tf_op jit(solution)/shard_map/qd,kd->qk/dot_general | solution.py:130
  159.6 9.2 %fusion = f32[1024]{0:T(1024)S(1)} fusion(f32[1024,4096]{1,0:T(8,128)} %get-tuple-element.39, f32[1024]{0:T(1024)S(1)} %get-tuple-element.38), kind=kLoop, calls=%fused_computation.5 | loop fusion | flops 12581888 | bytes 16785408 | tf_op jit(solution)/shard_map/reduce_sum | solution.py:131
  168.7 8.4 %fusion.18 = bf16[1024,128]{0,1:T(8,128)(2,1)S(1)} fusion(f32[1024,4096]{1,0:T(8,128)} %get-tuple-element.39, f32[1024]{0:T(1024)S(1)} %fusion, f32[1024]{0:T(1024)S(1)} %get-tuple-element.38, bf16[4096,256]{0,1:T(8,128)(2,1)} %all-gather.15.cloned.1.call-done), kind=kOutput, calls=%fused_computation.51 | convolution fusion | flops 1090650112 | bytes 18096128 | tf_op jit(solution)/shard_map/dot_general | solution.py:32
  177.2 2.8 collective-permute-start.13
  180.0 4.6 all-gather.21.cloned.1.call-done
  184.6 7.3 %fusion.4 = f32[1024,384]{0,1:T(8,128)} fusion(bf16[3072,384]{1,0:T(8,128)(2,1)} %all-gather.21.cloned.1.call-done, bf16[512,3072]{1,0:T(8,128)(2,1)} %bitcast.82, bf16[512,3072]{1,0:T(8,128)(2,1)} %copy-done.8), kind=kOutput, calls=%fused_computation.13 | convolution fusion | flops 2428502016 | bytes 10223616 | tf_op jit(solution)/shard_map/dot_general | solution.py:32
  194.8 25.1 %all-gather.19.cloned.1.call-done = bf16[3072,384]{1,0:T(8,128)(2,1)} async-done(((bf16[768,384]{1,0:T(8,128)(2,1)}), bf16[3072,384]{1,0:T(8,128)(2,1)}) %all-gather.19.cloned.1.call-update) | async-done | bytes 2359312 | tf_op jit(solution)/shard_map/all_gather | solution.py:104
  219.9 10.0 %fusion.10 = bf16[1024,384]{0,1:T(8,128)(2,1)S(1)} fusion(f32[1024,384]{0,1:T(8,128)} %fusion.4, f32[384]{0:T(512)S(1)} %dynamic_slice.123, bf16[3072,384]{1,0:T(8,128)(2,1)} %all-gather.19.cloned.1.call-done, bf16[512,3072]{1,0:T(8,128)(2,1)} %bitcast.80, bf16[512,3072]{1,0:T(8,128)(2,1)} %copy-done.7), kind=kOutput, calls=%fused_computation.28 | convolution fusion | flops 2454847488 | bytes 11011584 | tf_op jit(solution)/shard_map/dot_general | solution.py:32
  230.0 2.8 collective-permute-start.15
  232.7 8.8 %collective-permute-done.15 = bf16[512,384]{0,1:T(8,128)(2,1)S(1)} collective-permute-done((bf16[512,384]{0,1:T(8,128)(2,1)S(1)}, bf16[512,384]{0,1:T(8,128)(2,1)S(1)}, u32[]{:S(2)}, u32[]{:S(2)}) %collective-permute-start.15) | collective-permute-done | bytes 393248 | tf_op jit(solution)/shard_map/ppermute | solution.py:19
  242.7 2.3 copy.44
  245.1 2.9 collective-permute-start.22
  248.7 4.0 all-to-all-start.1
  252.8 2.9 collective-permute-start.21
  255.7 19.3 %all-to-all-done.1 = bf16[8,32,384]{2,1,0:T(8,128)(2,1)} async-done(((bf16[8,32,384]{2,1,0:T(8,128)(2,1)}), bf16[8,32,384]{2,1,0:T(8,128)(2,1)}, u32[]{:S(2)}, u32[]{:S(2)}) %all-to-all-start.1) | async-done | bytes 196640 | tf_op jit(solution)/shard_map/all_to_all | solution.py:139
  275.0 2.3 constant_dynamic-slice_fusion.5
  277.3 11.2 %all-gather.23.cloned.1.call-done = bf16[4,512,768]{2,1,0:T(8,128)(2,1)} async-done(((bf16[1,512,768]{2,1,0:T(8,128)(2,1)}), bf16[4,512,768]{2,1,0:T(8,128)(2,1)}) %all-gather.23.cloned.1.call-update) | async-done | bytes 3145744 | tf_op jit(solution)/shard_map/all_gather | solution.py:125
  292.1 2.7 fusion.40
  299.5 2.7 fusion.39
  305.8 2.5 collective-permute-start.25
  315.4 3.5 all-to-all-start
  322.1 6.5 %collective-permute-start.26 = (bf16[4,64,768]{2,1,0:T(8,128)(2,1)}, bf16[4,64,768]{2,1,0:T(8,128)(2,1)}, u32[]{:S(2)}, u32[]{:S(2)}) collective-permute-start(bf16[4,64,768]{2,1,0:T(8,128)(2,1)} %add_convert_fusion.2), channel_id=1, source_target_pairs={{0,2},{2,0},{4,6},{6,4},{1,3},{3,1},{5,7},{7,5},{8,10},{10,8},{12,... | collective-permute-start | bytes 1179656 | tf_op jit(solution)/shard_map/ppermute | solution.py:19
  333.6 3.4 collective-permute-done.26
  339.8 5.6 %collective-permute-done.17 = bf16[4,64,768]{2,1,0:T(8,128)(2,1)} collective-permute-done((bf16[4,64,768]{2,1,0:T(8,128)(2,1)}, bf16[4,64,768]{2,1,0:T(8,128)(2,1)}, u32[]{:S(2)}, u32[]{:S(2)}) %collective-permute-start.17) | collective-permute-done | bytes 393248 | tf_op jit(solution)/shard_map/ppermute | solution.py:19
  348.3 2.7 collective-permute-start.28
  351.6 6.2 %collective-permute-done.28 = bf16[4,32,768]{2,1,0:T(8,128)(2,1)S(1)} collective-permute-done((bf16[4,32,768]{2,1,0:T(8,128)(2,1)S(1)}, bf16[4,32,768]{2,1,0:T(8,128)(2,1)S(1)}, u32[]{:S(2)}, u32[]{:S(2)}) %collective-permute-start.28) | collective-permute-done | bytes 196640 | tf_op jit(solution)/shard_map/ppermute | solution.py:19
  360.4 3.2 collective-permute-start.30
  366.1 79.3 %all-gather.25.cloned.1.call-done = bf16[4096,384]{1,0:T(8,128)(2,1)} async-done(((bf16[512,384]{1,0:T(8,128)(2,1)}), bf16[4096,384]{1,0:T(8,128)(2,1)}) %all-gather.25.cloned.1.call-update) | async-done | bytes 3145744 | tf_op jit(solution)/shard_map/all_gather | solution.py:192
  445.4 5.5 %convolution_multiply_fusion.1 = f32[384,384]{1,0:T(8,128)} fusion(bf16[4096,384]{1,0:T(8,128)(2,1)} %all-gather.25.cloned.1.call-done, bf16[4096,384]{1,0:T(8,128)(2,1)} %bitcast.98), kind=kOutput, calls=%fused_computation.50 | convolution fusion | flops 1208107008 | bytes 6881280 | tf_op jit(solution)/shard_map/ti,tj->ij/dot_general | solution.py:197
  450.9 37.5 %all-gather.27.cloned.1.call-done = bf16[4096,768]{1,0:T(8,128)(2,1)} async-done(((bf16[256,768]{1,0:T(8,128)(2,1)}), bf16[4096,768]{1,0:T(8,128)(2,1)}) %all-gather.27.cloned.1.call-update) | async-done | bytes 6291472 | tf_op jit(solution)/shard_map/all_gather | solution.py:182
  488.4 7.4 %convolution_multiply_fusion = f32[384,768]{1,0:T(8,128)} fusion(bf16[4096,384]{1,0:T(8,128)(2,1)} %all-gather.25.cloned.1.call-done, bf16[4096,768]{1,0:T(8,128)(2,1)} %all-gather.27.cloned.1.call-done), kind=kOutput, calls=%fused_computation.49 | convolution fusion | flops 2416214016 | bytes 10616832 | tf_op jit(solution)/shard_map/ti,tj->ij/dot_general | solution.py:195
  (167 shorter events, 88.7 us)
Async XLA Ops:
  7.2 240.8 %copy-start = (bf16[512,3072]{1,0:T(8,128)(2,1)S(1)}, bf16[512,3072]{1,0:T(8,128)(2,1)}, u32[]{:S(2)}) copy-start(bf16[512,3072]{1,0:T(8,128)(2,1)} %param.19) | copy-start | bytes 9437188
  7.2 96.1 %all-gather.13.cloned.1.call-start = ((), (), s32[]{:S(2)}) async-start(), calls=%async_computation.3 | async-start | bytes 2949120 | tf_op jit(solution)/shard_map/all_gather | solution.py:78
  9.8 18.5 %copy-start.12 = (f32[6144]{0:T(1024)S(1)}, f32[6144]{0:T(1024)}, u32[]{:S(2)}) copy-start(f32[6144]{0:T(1024)} %param.11) | copy-start | bytes 73732
  11.9 16.2 %collective-permute-start.12 = (bf16[768,384]{0,1:T(8,128)(2,1)S(1)}, bf16[768,384]{0,1:T(8,128)(2,1)}, u32[]{:S(2)}, u32[]{:S(2)}) collective-permute-start(bf16[768,384]{0,1:T(8,128)(2,1)S(1)} %bitcast.95), channel_id=1, source_target_pairs={{0,64},{64,0},{1,65},{65,1},{2,66},{66,2},{3,67},{67,3},{4,68},{68... | collective-permute-start | bytes 1769480 | tf_op jit(solution)/shard_map/ppermute | solution.py:19
  28.2 82.4 %all-gather.11.cloned.1.call-start = ((), (), s32[]{:S(2)}) async-start(), calls=%async_computation.2 | async-start | bytes 2949120 | tf_op jit(solution)/shard_map/all_gather | solution.py:77
  39.2 10.9 %collective-permute-start.6 = (bf16[64,3072]{1,0:T(8,128)(2,1)S(1)}, bf16[64,3072]{1,0:T(8,128)(2,1)}, u32[]{:S(2)}, u32[]{:S(2)}) collective-permute-start(bf16[64,3072]{1,0:T(8,128)(2,1)S(1)} %constant_dynamic-slice_fusion.11), channel_id=1, source_target_pairs={{0,64},{64,0},{1,65},{65,1},{2,66},{66,2},{3,67},{67,3},{4,68},{68... | collective-permute-start | bytes 1179656 | tf_op jit(solution)/shard_map/ppermute | solution.py:19
  43.2 15.4 %collective-permute-start = (bf16[64,3072]{1,0:T(8,128)(2,1)}, bf16[64,3072]{1,0:T(8,128)(2,1)}, u32[]{:S(2)}, u32[]{:S(2)}) collective-permute-start(bf16[64,3072]{1,0:T(8,128)(2,1)} %constant_dynamic-slice_fusion.13), channel_id=1, source_target_pairs={{0,64},{64,0},{1,65},{65,1},{2,66},{66,2},{3,67},{67,3},{4,68},{68... | collective-permute-start | bytes 1179656 | tf_op jit(solution)/shard_map/ppermute | solution.py:19
  50.2 14.6 %collective-permute-start.9 = (bf16[64,3072]{1,0:T(8,128)(2,1)}, bf16[64,3072]{1,0:T(8,128)(2,1)S(1)}, u32[]{:S(2)}, u32[]{:S(2)}) collective-permute-start(bf16[64,3072]{1,0:T(8,128)(2,1)} %collective-permute-done.6), channel_id=1, source_target_pairs={{0,6},{2,0},{4,2},{6,4},{1,7},{3,1},{5,3},{7,5},{8,14},{10,8},{12,... | collective-permute-start | bytes 1179656 | tf_op jit(solution)/shard_map/ppermute | solution.py:24
  53.1 13.2 %collective-permute-start.7 = (bf16[64,3072]{1,0:T(8,128)(2,1)}, bf16[64,3072]{1,0:T(8,128)(2,1)}, u32[]{:S(2)}, u32[]{:S(2)}) collective-permute-start(bf16[64,3072]{1,0:T(8,128)(2,1)} %collective-permute-done.6), channel_id=1, source_target_pairs={{0,2},{2,4},{4,6},{6,0},{1,3},{3,5},{5,7},{7,1},{8,10},{10,12},{12... | collective-permute-start | bytes 1179656 | tf_op jit(solution)/shard_map/ppermute | solution.py:24
  53.1 96.8 %all-gather.15.cloned.1.call-start = ((), (), s32[]{:S(2)}) async-start(), calls=%async_computation.4 | async-start | bytes 2621440 | tf_op jit(solution)/shard_map/all_gather | solution.py:113
  58.6 26.0 %collective-permute-start.1 = (bf16[64,3072]{1,0:T(8,128)(2,1)}, bf16[64,3072]{1,0:T(8,128)(2,1)S(1)}, u32[]{:S(2)}, u32[]{:S(2)}) collective-permute-start(bf16[64,3072]{1,0:T(8,128)(2,1)} %collective-permute-done), channel_id=1, source_target_pairs={{0,2},{2,4},{4,6},{6,0},{1,3},{3,5},{5,7},{7,1},{8,10},{10,12},{12... | collective-permute-start | bytes 1179656 | tf_op jit(solution)/shard_map/ppermute | solution.py:24
  60.1 24.4 %collective-permute-start.3 = (bf16[64,3072]{1,0:T(8,128)(2,1)}, bf16[64,3072]{1,0:T(8,128)(2,1)S(1)}, u32[]{:S(2)}, u32[]{:S(2)}) collective-permute-start(bf16[64,3072]{1,0:T(8,128)(2,1)} %collective-permute-done), channel_id=1, source_target_pairs={{0,6},{2,0},{4,2},{6,4},{1,7},{3,1},{5,3},{7,5},{8,14},{10,8},{12,... | collective-permute-start | bytes 1179656 | tf_op jit(solution)/shard_map/ppermute | solution.py:24
  64.7 8.7 %collective-permute-start.10 = (bf16[32,3072]{1,0:T(8,128)(2,1)S(1)}, bf16[32,3072]{1,0:T(8,128)(2,1)S(1)}, u32[]{:S(2)}, u32[]{:S(2)}) collective-permute-start(bf16[32,3072]{1,0:T(8,128)(2,1)S(1)} %slice.64), channel_id=1, source_target_pairs={{0,6},{2,0},{4,2},{6,4},{1,7},{3,1},{5,3},{7,5},{8,14},{10,8},{12,... | collective-permute-start | bytes 589832 | tf_op jit(solution)/shard_map/ppermute | solution.py:24
  67.3 8.3 %collective-permute-start.8 = (bf16[32,3072]{1,0:T(8,128)(2,1)S(1)}, bf16[32,3072]{1,0:T(8,128)(2,1)S(1)}, u32[]{:S(2)}, u32[]{:S(2)}) collective-permute-start(bf16[32,3072]{1,0:T(8,128)(2,1)S(1)} %slice.63), channel_id=1, source_target_pairs={{0,2},{2,4},{4,6},{6,0},{1,3},{3,5},{5,7},{7,1},{8,10},{10,12},{12... | collective-permute-start | bytes 589832 | tf_op jit(solution)/shard_map/ppermute | solution.py:24
  77.1 17.9 %collective-permute-start.11 = (bf16[256,3072]{1,0:T(8,128)(2,1)}, bf16[256,3072]{1,0:T(8,128)(2,1)}, u32[]{:S(2)}, u32[]{:S(2)}) collective-permute-start(bf16[256,3072]{1,0:T(8,128)(2,1)} %constant_dynamic-update-slice_fusion), channel_id=1, source_target_pairs={{0,1},{1,0},{2,3},{3,2},{4,5},{5,4},{6,7},{7,6},{8,9},{9,8},{10,11... | collective-permute-start | bytes 4718600 | tf_op jit(solution)/shard_map/ppermute | solution.py:19
  84.5 10.5 %copy-start.14 = (f32[2,128]{1,0:T(2,128)S(1)}, f32[2,128]{1,0:T(2,128)}, u32[]{:S(2)}) copy-start(f32[2,128]{1,0:T(2,128)} %param.13) | copy-start | bytes 3076
  84.5 6.7 %collective-permute-start.4 = (bf16[32,3072]{1,0:T(8,128)(2,1)S(1)}, bf16[32,3072]{1,0:T(8,128)(2,1)S(1)}, u32[]{:S(2)}, u32[]{:S(2)}) collective-permute-start(bf16[32,3072]{1,0:T(8,128)(2,1)S(1)} %slice.62), channel_id=1, source_target_pairs={{0,6},{2,0},{4,2},{6,4},{1,7},{3,1},{5,3},{7,5},{8,14},{10,8},{12,... | collective-permute-start | bytes 589832 | tf_op jit(solution)/shard_map/ppermute | solution.py:24
  84.6 7.9 %collective-permute-start.2 = (bf16[32,3072]{1,0:T(8,128)(2,1)S(1)}, bf16[32,3072]{1,0:T(8,128)(2,1)S(1)}, u32[]{:S(2)}, u32[]{:S(2)}) collective-permute-start(bf16[32,3072]{1,0:T(8,128)(2,1)S(1)} %slice.61), channel_id=1, source_target_pairs={{0,2},{2,4},{4,6},{6,0},{1,3},{3,5},{5,7},{7,1},{8,10},{10,12},{12... | collective-permute-start | bytes 589832 | tf_op jit(solution)/shard_map/ppermute | solution.py:24
  94.1 5.1 %collective-permute-start.5 = (bf16[256,3072]{1,0:T(8,128)(2,1)}, bf16[256,3072]{1,0:T(8,128)(2,1)}, u32[]{:S(2)}, u32[]{:S(2)}) collective-permute-start(bf16[256,3072]{1,0:T(8,128)(2,1)} %constant_dynamic-update-slice_fusion.3), channel_id=1, source_target_pairs={{0,1},{1,0},{2,3},{3,2},{4,5},{5,4},{6,7},{7,6},{8,9},{9,8},{10,11... | collective-permute-start | bytes 4718600 | tf_op jit(solution)/shard_map/ppermute | solution.py:19
  119.2 65.4 %all-gather.21.cloned.1.call-start = ((), (), s32[]{:S(2)}) async-start(), calls=%async_computation.7 | async-start | bytes 2949120 | tf_op jit(solution)/shard_map/all_gather | solution.py:105
  119.2 19.9 %copy-start.13 = (f32[768]{0:T(1024)S(1)}, f32[768]{0:T(1024)}, u32[]{:S(2)}) copy-start(f32[768]{0:T(1024)} %param.15) | copy-start | bytes 9220
  121.4 16.5 %collective-permute-start.14 = (bf16[768,384]{1,0:T(8,128)(2,1)S(1)}, bf16[768,384]{1,0:T(8,128)(2,1)}, u32[]{:S(2)}, u32[]{:S(2)}) collective-permute-start(bf16[768,384]{1,0:T(8,128)(2,1)S(1)} %get-tuple-element.21), channel_id=1, source_target_pairs={{0,64},{64,0},{1,65},{65,1},{2,66},{66,2},{3,67},{67,3},{4,68},{68... | collective-permute-start | bytes 1769480 | tf_op jit(solution)/shard_map/ppermute | solution.py:19
  138.0 81.9 %all-gather.19.cloned.1.call-start = ((), (), s32[]{:S(2)}) async-start(), calls=%async_computation.6 | async-start | bytes 2949120 | tf_op jit(solution)/shard_map/all_gather | solution.py:104
  138.6 136.5 %all-gather.17.cloned.1.call-start = ((), (), s32[]{:S(2)}) async-start(), calls=%async_computation.5 | async-start | bytes 1310720 | tf_op jit(solution)/shard_map/all_gather | solution.py:125
  177.2 14.8 %collective-permute-start.13 = (bf16[512,128]{0,1:T(8,128)(2,1)S(1)}, bf16[512,128]{0,1:T(8,128)(2,1)S(1)}, u32[]{:S(2)}, u32[]{:S(2)}) collective-permute-start(bf16[512,128]{0,1:T(8,128)(2,1)S(1)} %get-tuple-element.31), channel_id=1, source_target_pairs={{0,64},{64,0},{1,65},{65,1},{2,66},{66,2},{3,67},{67,3},{4,68},{68... | collective-permute-start | bytes 393224 | tf_op jit(solution)/shard_map/ppermute | solution.py:19
  194.5 93.9 %all-gather.23.cloned.1.call-start = ((), (), s32[]{:S(2)}) async-start(), calls=%async_computation.8 | async-start | bytes 3932160 | tf_op jit(solution)/shard_map/all_gather | solution.py:125
  230.0 11.6 %collective-permute-start.15 = (bf16[512,384]{0,1:T(8,128)(2,1)S(1)}, bf16[512,384]{0,1:T(8,128)(2,1)S(1)}, u32[]{:S(2)}, u32[]{:S(2)}) collective-permute-start(bf16[512,384]{0,1:T(8,128)(2,1)S(1)} %get-tuple-element.25), channel_id=1, source_target_pairs={{0,64},{64,0},{1,65},{65,1},{2,66},{66,2},{3,67},{67,3},{4,68},{68... | collective-permute-start | bytes 1179656 | tf_op jit(solution)/shard_map/ppermute | solution.py:19
  245.1 47.0 %collective-permute-start.22 = (bf16[768,768]{1,0:T(8,128)(2,1)}, bf16[768,768]{1,0:T(8,128)(2,1)}, u32[]{:S(2)}, u32[]{:S(2)}) collective-permute-start(bf16[768,768]{1,0:T(8,128)(2,1)} %param.17), channel_id=1, source_target_pairs={{0,64},{64,0},{1,65},{65,1},{2,66},{66,2},{3,67},{67,3},{4,68},{68... | collective-permute-start | bytes 3538952 | tf_op jit(solution)/shard_map/ppermute | solution.py:19
  248.7 26.3 %all-to-all-start.1 = ((bf16[8,32,384]{2,1,0:T(8,128)(2,1)}), bf16[8,32,384]{2,1,0:T(8,128)(2,1)}, u32[]{:S(2)}, u32[]{:S(2)}) async-start(bf16[8,32,384]{2,1,0:T(8,128)(2,1)} %copy.46), calls=%async_computation.1 | async-start | bytes 393216 | tf_op jit(solution)/shard_map/all_to_all | solution.py:139
  252.7 113.4 %all-gather.29.cloned.1.call-start = ((), (), s32[]{:S(2)}) async-start(), calls=%async_computation.11 | async-start | bytes 3342336 | tf_op jit(solution)/shard_map/all_gather | solution.py:140
  252.8 42.0 %collective-permute-start.21 = (bf16[256,768]{1,0:T(8,128)(2,1)S(1)}, bf16[256,768]{1,0:T(8,128)(2,1)}, u32[]{:S(2)}, u32[]{:S(2)}) collective-permute-start(bf16[256,768]{1,0:T(8,128)(2,1)S(1)} %copy-done.9), channel_id=1, source_target_pairs={{0,64},{64,0},{1,65},{65,1},{2,66},{66,2},{3,67},{67,3},{4,68},{68... | collective-permute-start | bytes 1179656 | tf_op jit(solution)/shard_map/ppermute | solution.py:19
  296.4 8.0 %collective-permute-start.23 = (bf16[4,256,768]{2,1,0:T(8,128)(2,1)S(1)}, bf16[4,256,768]{2,1,0:T(8,128)(2,1)S(1)}, u32[]{:S(2)}, u32[]{:S(2)}) collective-permute-start(bf16[4,256,768]{2,1,0:T(8,128)(2,1)S(1)} %bitcast.88), channel_id=1, source_target_pairs={{0,1},{1,0},{2,3},{3,2},{4,5},{5,4},{6,7},{7,6},{8,9},{9,8},{10,11... | collective-permute-start | bytes 4718600 | tf_op jit(solution)/shard_map/ppermute | solution.py:19
  297.7 10.5 %collective-permute-start.16 = (bf16[4,256,768]{2,1,0:T(8,128)(2,1)S(1)}, bf16[4,256,768]{2,1,0:T(8,128)(2,1)S(1)}, u32[]{:S(2)}, u32[]{:S(2)}) collective-permute-start(bf16[4,256,768]{2,1,0:T(8,128)(2,1)S(1)} %bitcast.87), channel_id=1, source_target_pairs={{0,1},{1,0},{2,3},{3,2},{4,5},{5,4},{6,7},{7,6},{8,9},{9,8},{10,11... | collective-permute-start | bytes 4718600 | tf_op jit(solution)/shard_map/ppermute | solution.py:19
  305.8 14.2 %collective-permute-start.25 = (bf16[4,64,768]{2,1,0:T(8,128)(2,1)}, bf16[4,64,768]{2,1,0:T(8,128)(2,1)}, u32[]{:S(2)}, u32[]{:S(2)}) collective-permute-start(bf16[4,64,768]{2,1,0:T(8,128)(2,1)} %get-tuple-element.11), channel_id=1, source_target_pairs={{0,6},{2,4},{4,2},{6,0},{1,7},{3,5},{5,3},{7,1},{8,14},{10,12},{12... | collective-permute-start | bytes 1179656 | tf_op jit(solution)/shard_map/ppermute | solution.py:19
  311.2 18.3 %collective-permute-start.18 = (bf16[4,64,768]{2,1,0:T(8,128)(2,1)}, bf16[4,64,768]{2,1,0:T(8,128)(2,1)}, u32[]{:S(2)}, u32[]{:S(2)}) collective-permute-start(bf16[4,64,768]{2,1,0:T(8,128)(2,1)} %get-tuple-element.9), channel_id=1, source_target_pairs={{0,2},{2,0},{4,6},{6,4},{1,3},{3,1},{5,7},{7,5},{8,10},{10,8},{12,... | collective-permute-start | bytes 1179656 | tf_op jit(solution)/shard_map/ppermute | solution.py:19
  315.4 17.4 %all-to-all-start = ((bf16[4,32,2,768]{3,2,1,0:T(2,128)(2,1)}), bf16[4,32,2,768]{3,2,1,0:T(2,128)(2,1)S(1)}, u32[]{:S(2)}, u32[]{:S(2)}) async-start(bf16[4,32,2,768]{3,2,1,0:T(2,128)(2,1)} %copy.40), calls=%async_computation | async-start | bytes 786432 | tf_op jit(solution)/shard_map/all_to_all | solution.py:137
  318.9 126.6 %all-gather.25.cloned.1.call-start = ((), (), s32[]{:S(2)}) async-start(), calls=%async_computation.9 | async-start | bytes 3538944 | tf_op jit(solution)/shard_map/all_gather | solution.py:192
  318.9 14.7 %collective-permute-start.24 = (bf16[4,64,768]{2,1,0:T(8,128)(2,1)}, bf16[4,64,768]{2,1,0:T(8,128)(2,1)}, u32[]{:S(2)}, u32[]{:S(2)}) collective-permute-start(bf16[4,64,768]{2,1,0:T(8,128)(2,1)} %get-tuple-element.10), channel_id=1, source_target_pairs={{0,6},{2,4},{4,2},{6,0},{1,7},{3,5},{5,3},{7,1},{8,14},{10,12},{12... | collective-permute-start | bytes 1179656 | tf_op jit(solution)/shard_map/ppermute | solution.py:19
  322.1 14.9 %collective-permute-start.26 = (bf16[4,64,768]{2,1,0:T(8,128)(2,1)}, bf16[4,64,768]{2,1,0:T(8,128)(2,1)}, u32[]{:S(2)}, u32[]{:S(2)}) collective-permute-start(bf16[4,64,768]{2,1,0:T(8,128)(2,1)} %add_convert_fusion.2), channel_id=1, source_target_pairs={{0,2},{2,0},{4,6},{6,4},{1,3},{3,1},{5,7},{7,5},{8,10},{10,8},{12,... | collective-permute-start | bytes 1179656 | tf_op jit(solution)/shard_map/ppermute | solution.py:19
  329.4 16.0 %collective-permute-start.17 = (bf16[4,64,768]{2,1,0:T(8,128)(2,1)}, bf16[4,64,768]{2,1,0:T(8,128)(2,1)}, u32[]{:S(2)}, u32[]{:S(2)}) collective-permute-start(bf16[4,64,768]{2,1,0:T(8,128)(2,1)} %get-tuple-element.8), channel_id=1, source_target_pairs={{0,2},{2,0},{4,6},{6,4},{1,3},{3,1},{5,7},{7,5},{8,10},{10,8},{12,... | collective-permute-start | bytes 1179656 | tf_op jit(solution)/shard_map/ppermute | solution.py:19
  331.6 13.8 %collective-permute-start.19 = (bf16[4,64,768]{2,1,0:T(8,128)(2,1)}, bf16[4,64,768]{2,1,0:T(8,128)(2,1)}, u32[]{:S(2)}, u32[]{:S(2)}) collective-permute-start(bf16[4,64,768]{2,1,0:T(8,128)(2,1)} %add_convert_fusion.3), channel_id=1, source_target_pairs={{0,6},{2,4},{4,2},{6,0},{1,7},{3,5},{5,3},{7,1},{8,14},{10,12},{12... | collective-permute-start | bytes 1179656 | tf_op jit(solution)/shard_map/ppermute | solution.py:19
  338.5 9.7 %collective-permute-start.27 = (bf16[4,32,768]{2,1,0:T(8,128)(2,1)S(1)}, bf16[4,32,768]{2,1,0:T(8,128)(2,1)S(1)}, u32[]{:S(2)}, u32[]{:S(2)}) collective-permute-start(bf16[4,32,768]{2,1,0:T(8,128)(2,1)S(1)} %dynamic-slice_convert_fusion.4), channel_id=1, source_target_pairs={{0,8},{8,0},{1,9},{9,1},{2,10},{10,2},{3,11},{11,3},{4,12},{12,4},... | collective-permute-start | bytes 589832 | tf_op jit(solution)/shard_map/ppermute | solution.py:19
  346.9 4.6 collective-permute-start.20
  348.3 9.5 %collective-permute-start.28 = (bf16[4,32,768]{2,1,0:T(8,128)(2,1)S(1)}, bf16[4,32,768]{2,1,0:T(8,128)(2,1)S(1)}, u32[]{:S(2)}, u32[]{:S(2)}) collective-permute-start(bf16[4,32,768]{2,1,0:T(8,128)(2,1)S(1)} %fusion.23), channel_id=1, source_target_pairs={{0,64},{64,0},{1,65},{65,1},{2,66},{66,2},{3,67},{67,3},{4,68},{68... | collective-permute-start | bytes 589832 | tf_op jit(solution)/shard_map/ppermute | solution.py:19
  357.9 8.0 %copy-start.10 = (bf16[8,32,768]{2,1,0:T(8,128)(2,1)}, bf16[8,32,768]{2,1,0:T(8,128)(2,1)S(1)}, u32[]{:S(2)}) copy-start(bf16[8,32,768]{2,1,0:T(8,128)(2,1)S(1)} %maximum_select_fusion.1) | copy-start | bytes 1179652
  357.9 1.4 collective-permute-start.29
  360.4 4.2 collective-permute-start.30
  365.5 122.9 %all-gather.27.cloned.1.call-start = ((), (), s32[]{:S(2)}) async-start(), calls=%async_computation.10 | async-start | bytes 6684672 | tf_op jit(solution)/shard_map/all_gather | solution.py:182
  (11 other events, 33.9 us)
Sparse Core Ops, SparseCore 0:
  28.3 36.8 all-gather.12
  67.4 33.1 all-gather.10
  119.3 30.5 all-gather.14
  151.5 33.0 all-gather.20
  186.7 33.1 all-gather.18
  221.4 23.1 all-gather.16
  246.3 42.1 all-gather.22
  290.2 40.8 all-gather.28
  365.6 79.7 all-gather.24
  447.6 40.8 all-gather.26

commit v2 on v1

v2 whole, which is shorter than its diff:
```python
import jax
import jax.numpy as jnp
from jax import lax
from jax.sharding import Mesh, PartitionSpec as P

HEAD = 128
BF = jnp.bfloat16
F32 = jnp.float32


def layer_norm(inputs, norm_scale):
    center = jnp.mean(inputs, axis=-1, keepdims=True)
    spread = jnp.mean(jnp.square(inputs - center), axis=-1, keepdims=True)
    return (inputs - center) * lax.rsqrt(spread + 1e-06) * norm_scale


def swap(x, axis, mask):
    size = lax.axis_size(axis)
    return lax.ppermute(x, axis, [(i, i ^ mask) for i in range(size)])


def shift(x, axis, step):
    size = lax.axis_size(axis)
    return lax.ppermute(x, axis, [(i, (i + step) % size) for i in range(size)])


def dyn(x, start, size, axis):
    return lax.dynamic_slice_in_dim(x, start, size, axis)


def dot(a, b):
    return jnp.dot(a, b, preferred_element_type=F32)


def ring_gather(x, axis):
    below = shift(x, axis, 1)
    above = shift(x, axis, -1)
    half = x.shape[0] // 2
    far_low = shift(below[:half], axis, 1)
    far_high = shift(above[half:], axis, -1)
    return [x, above, jnp.concatenate([far_low, far_high]), below]


def in_order(blocks, index):
    count = len(blocks)
    laid = [lax.select_n(lax.rem(i - index + count, count), *blocks) for i in range(count)]
    return jnp.concatenate(laid)


def both(flag, first, second, axis=0):
    return jnp.where(
        flag == 0,
        jnp.concatenate([first, second], axis=axis),
        jnp.concatenate([second, first], axis=axis),
    )


def on_device(
    tokens,
    norm_gain,
    qkv_weight,
    qk_gains,
    in_weight,
    in_bias,
    out_weight,
    mlp_out_weight,
    out_bias,
    targets,
):
    xh, z, xl, y, c = (lax.axis_index(a) for a in ("xh", "z", "xl", "y", "c"))
    rows, width = tokens.shape
    half = width // 2
    block = width // 8
    target_block = targets.shape[1] // 8
    piece = rows // 16

    qkv_rows = lax.all_gather(qkv_weight.reshape(block, 6 * HEAD), "z", axis=0, tiled=True)
    in_rows = lax.all_gather(in_weight, "z", axis=0, tiled=True)

    at = ((c * 4 + y) * 2 + xl) * piece
    base_rows = dyn(tokens, at, piece, 0).reshape(piece, 8, block)
    goal_rows = dyn(targets, at, piece, 0).reshape(piece, 8, target_block)
    spread_rows = jnp.concatenate([base_rows, goal_rows], axis=2).transpose(1, 0, 2)
    own_spread = lax.all_to_all(spread_rows, ("xh", "z"), split_axis=0, concat_axis=0, tiled=True)

    token_values = tokens.astype(F32)
    center = jnp.mean(token_values, axis=-1, keepdims=True)
    spread = jnp.mean(jnp.square(token_values - center), axis=-1, keepdims=True)
    scale = lax.rsqrt(spread + 1e-06)

    def normed_part(start, count, which):
        part = dyn(dyn(tokens, start, count, 0), which * half, half, 1).astype(F32)
        gain = dyn(norm_gain, which * half, half, 0)
        shift_rows, scale_rows = dyn(center, start, count, 0), dyn(scale, start, count, 0)
        return ((part - shift_rows) * scale_rows * gain).astype(BF)

    share = rows // 8
    got = swap(normed_part((c * 4 + y) * share, share, 1 - xh), "xh", 1)
    norm_own = normed_part(0, rows, xh)
    got, out_weight, mlp_out_weight = lax.optimization_barrier((got, out_weight, mlp_out_weight))
    around = in_order(ring_gather(got, "y"), y)
    norm_far = both(c, around, swap(around, "c", 1))

    far_out, far_mlp = swap(out_weight, "xh", 1), swap(mlp_out_weight, "xh", 1)

    qkv_own = dot(norm_own, qkv_rows).reshape(rows, 3, 2, HEAD)
    qkv_far = dot(norm_far, qkv_rows).reshape(rows, 3, 2, HEAD)

    def head_of(x, which):
        return dyn(x, which, 1, 2).reshape(rows, 3 * HEAD)

    give = jnp.concatenate([head_of(qkv_far, 1 - xh), head_of(qkv_own, 1 - xh)]).astype(BF)
    keep = jnp.concatenate([head_of(qkv_own, xh), head_of(qkv_far, xh)])
    qkv = keep + swap(give, "xh", 1).astype(F32)
    queries = layer_norm(qkv[:, :HEAD], qk_gains[0]).astype(BF)
    own_keys = layer_norm(qkv[:, HEAD : 2 * HEAD], qk_gains[1]).astype(BF)
    own_kv = jnp.concatenate([own_keys, qkv[:, 2 * HEAD :].astype(BF)], axis=1)
    all_kv = jnp.concatenate(ring_gather(own_kv, "z"))

    mlp_far = swap(dot(norm_far, in_rows).astype(BF), "xh", 1)
    mlp_input = dot(norm_own, in_rows) + mlp_far.astype(F32)
    hidden = jax.nn.gelu(mlp_input + in_bias, approximate=False).astype(BF)
    hidden = jnp.stack(ring_gather(hidden, "z"))

    all_keys, all_values = all_kv[:, :HEAD], all_kv[:, HEAD:]
    scores = jnp.einsum("qd,kd->qk", queries, all_keys, preferred_element_type=F32) * HEAD ** (-0.5)
    soft_weights = jax.nn.softmax(scores, axis=-1).astype(BF)
    attended = dot(soft_weights, all_values).astype(BF)
    attended = both(xh, attended[:rows], swap(attended[rows:], "xh", 1), axis=1)
    attended = jnp.stack(ring_gather(attended, "z"))

    part_rows = rows // 2

    def partial(start, out_w, mlp_w):
        a = dyn(attended, start, part_rows, 1).reshape(4 * part_rows, -1)
        h = dyn(hidden, start, part_rows, 1).reshape(4 * part_rows, -1)
        return (dot(a, out_w) + dot(h, mlp_w)).reshape(4, part_rows, block)

    def over_core(out_w, mlp_w):
        give = partial((1 - c) * part_rows, out_w, mlp_w).astype(BF)
        got = swap(give, "c", 1)
        return partial(c * part_rows, out_w, mlp_w) + got.astype(F32)

    quarter = part_rows // 4

    def over_y(x, first, second):
        def at_index(i):
            return dyn(x, i * quarter, quarter, 1)

        third = first ^ second
        one = swap(at_index(y ^ third).astype(BF), "y", first)
        two = swap(at_index(y ^ first).astype(BF), "y", first)
        far = at_index(y ^ second) + one.astype(F32)
        return at_index(y) + two.astype(F32) + swap(far.astype(BF), "y", second).astype(F32)

    def over_xl(x):
        got = swap(dyn(x, (1 - xl) * piece, piece, 1).astype(BF), "xl", 1)
        return dyn(x, xl * piece, piece, 1) + got.astype(F32)

    sum_par = over_xl(over_y(over_core(far_out, far_mlp), 3, 1))
    sum_own = over_xl(over_y(over_core(out_weight, mlp_out_weight), 1, 3))
    theirs = swap(sum_par.astype(BF), "xh", 1).astype(F32)
    total = both(xh, in_order([sum_own[i] for i in range(4)], z), in_order([theirs[i] for i in range(4)], z))
    base = own_spread[:, :, :block].reshape(8 * piece, block).astype(F32)
    bias = dyn(out_bias, (xh * 4 + z) * block, block, 0)
    out_piece = (base + bias + total).astype(BF)

    turned = lax.ppermute(
        out_piece,
        ("xh", "z", "xl", "y"),
        [(a * 8 + b, b * 8 + a) for a in range(8) for b in range(8)],
    )
    narrow = block // 2
    stay = dyn(turned, c * narrow, narrow, 1)
    come = swap(dyn(turned, (1 - c) * narrow, narrow, 1), "c", 1)
    own_columns = lax.all_gather(both(c, stay, come), ("xh", "z"), axis=0, tiled=True)

    total_tokens = rows * 8
    over_xl_pair = both(xl, out_piece, swap(out_piece, "xl", 1))
    by_place = own_columns.reshape(2, 4, 16 * piece, narrow)
    gram = 0.0
    for distance, part in enumerate(ring_gather(over_xl_pair, "y")):
        other = swap(part, "c", 1)
        part, other = part.reshape(2, 8 * piece, block), other.reshape(2, 8 * piece, block)
        mine = dyn(by_place, lax.rem(y + distance, 4), 1, 1).reshape(2, 16 * piece, narrow)
        full = both(c, part, other, axis=1)
        gram = gram + jnp.einsum("ati,atj->ij", mine, full, preferred_element_type=F32)
    all_targets = lax.all_gather(own_spread[:, :, block:], ("xl", "y", "c"), axis=0, tiled=True)
    all_targets = all_targets.reshape(total_tokens, target_block)
    cross = jnp.einsum("ti,tj->ij", own_columns, all_targets, preferred_element_type=F32)
    return gram / total_tokens, cross / total_tokens


def solution(mesh):
    fine = Mesh(mesh.devices.reshape(2, 4, 2, 4, 2), ("xh", "z", "xl", "y", "c"))
    dp, mp = ("xh", "z"), ("xl", "y", "c")
    placed = (
        P(dp, None),
        P(),
        P(dp, None, mp),
        P(),
        P(dp, mp),
        P(mp),
        P(mp, dp),
        P(mp, dp),
        P(),
        P(dp, None),
    )
    return jax.shard_map(
        on_device,
        mesh=fine,
        in_specs=placed,
        out_specs=(P(mp, dp), P(mp, dp)),
        check_vma=False,
    )
```

time: 511 us -> 474 us (0.928)
  waiting for transfers between devices: 264 us -> 143 us
  starting transfers between devices: 67.2 us -> 98.6 us
  local copies, waits for them, and re-layouts: 42.1 us -> 72.3 us
  matrix products: 74.7 us -> 87 us
  other arithmetic: 39.7 us -> 51.3 us
    all_gather x10 -> x4, waiting for transfers between devices: 168 us -> 50.1 us  [the longest x1 23.2 us: on_device(): lax.all_gather(own_spread[:, :, block:], ('xl', 'y', 'c'), axis=0, tiled=...]
    ppermute x8 -> x20, waiting for transfers between devices: 12 us -> 47.5 us  [shift(): return lax.ppermute(x, axis, [(i, (i + step) % size) for i in range(size)])]
    ppermute x8 -> x20, starting transfers between devices: 9.15 us -> 40 us  [shift(): return lax.ppermute(x, axis, [(i, (i + step) % size) for i in range(size)])]
    ppermute x22 -> x24, waiting for transfers between devices: 63.4 us -> 44.4 us  [swap(): return lax.ppermute(x, axis, [(i, i ^ mask) for i in range(size)])]
    all_to_all x2 -> x1, waiting for transfers between devices: 19.3 us -> 0.92 us  [on_device(): lax.all_to_all(spread_rows, ('xh', 'z'), split_axis=0, concat_axis=0, til...]
    unnamed x34 -> x97, local copies, waits for them, and re-layouts: 8.03 us -> 24.2 us
    slice x4 -> x12, local copies, waits for them, and re-layouts: 0.98 us -> 11.8 us  [the longest x5 4.72 us: ring_gather(): far_high = shift(above[half:], axis, -1)]
    dynamic_slice x13, local copies, waits for them, and re-layouts: 14.1 us -> 24.1 us  [dyn(): return lax.dynamic_slice_in_dim(x, start, size, axis)]
  transfers between devices with their start and end apart: 43 -> 50, of which waited for: 21 -> 21; matrix products, arithmetic and copies ran while one was open for 26% -> 41% of each run, Pallas kernels for 0% -> 0%
where the time goes in v2:
time: 474 us; the launch traced here: 467 us
  waiting for transfers between devices  143 us (30%)
  starting transfers between devices  98.6 us (21%)
  matrix products  87 us (18%)
  local copies, waits for them, and re-layouts  72.3 us (15%)
  other arithmetic  51.3 us (11%)
  between operations  15 us (3%)
    dot_general x13, matrix products, dot(): return jnp.dot(a, b, preferred_element_type=F32)  60.6 us
    ppermute x24, starting transfers between devices, swap(): return lax.ppermute(x, axis, [(i, i ^ mask) for i in range(size)])  52.8 us
    ppermute x20, waiting for transfers between devices, shift(): return lax.ppermute(x, axis, [(i, (i + step) % size) for i in range(size)])  47.5 us
    ppermute x24, waiting for transfers between devices, swap(): return lax.ppermute(x, axis, [(i, i ^ mask) for i in range(size)])  44.4 us
    ppermute x20, starting transfers between devices, shift(): return lax.ppermute(x, axis, [(i, (i + step) % size) for i in range(size)])  40 us
    unnamed x97, local copies, waits for them, and re-layouts  24.2 us
    dynamic_slice x13, local copies, waits for them, and re-layouts, dyn(): return lax.dynamic_slice_in_dim(x, start, size, axis)  24.1 us
    all_gather x1, waiting for transfers between devices, on_device(): lax.all_gather(own_spread[:, :, block:], ('xl', 'y', 'c'), axis=0, tiled=...  23.2 us
  transfers between devices with their start and end apart: 50, of which 21 were waited for; matrix products, arithmetic and copies ran while one was open for 41% of the time, Pallas kernels for 0%

profile of v2, /device:TPU:1, one launch (start us, length us, event | category | flops | bytes accessed | tf_op | source)
XLA Modules:
  0.0 467.1 jit_solution(15666049707476003756)
XLA Ops:
  9.9 3.8 convert_reduce_fusion
  17.6 3.7 collective-permute-start
  21.2 8.5 %collective-permute-done = bf16[64,3072]{1,0:T(8,128)(2,1)} collective-permute-done((bf16[64,3072]{1,0:T(8,128)(2,1)S(1)}, bf16[64,3072]{1,0:T(8,128)(2,1)}, u32[]{:S(2)}, u32[]{:S(2)}) %collective-permute-start) | collective-permute-done | bytes 393248 | tf_op jit(solution)/shard_map/ppermute | solution.py:19
  32.8 8.1 %collective-permute-done.2 = bf16[64,3072]{1,0:T(8,128)(2,1)S(1)} collective-permute-done((bf16[64,3072]{1,0:T(8,128)(2,1)}, bf16[64,3072]{1,0:T(8,128)(2,1)S(1)}, u32[]{:S(2)}, u32[]{:S(2)}) %collective-permute-start.2) | collective-permute-done | bytes 393248 | tf_op jit(solution)/shard_map/ppermute | solution.py:24
  57.3 3.2 collective-permute-start.5
  63.8 3.6 constant_dynamic-update-slice_fusion.11
  70.6 7.1 %fusion.51 = f32[512,768]{1,0:T(8,128)} fusion(bf16[3072,768]{0,1:T(8,128)(2,1)} %all-gather.5.cloned.1.call-done, bf16[512,3072]{1,0:T(8,128)(2,1)} %get-tuple-element.43, bf16[512,3072]{1,0:T(8,128)(2,1)} %constant_dynamic-update-slice_fusion.7, pred[]{:T(512)S(6)} %eq.6), kind=kOutput, calls=%fused_computation.83 | convolution fusion | flops 2417491968 | bytes 12582913 | tf_op jit(solution)/shard_map/dot_general | solution.py:32
  77.7 3.0 reshape.279
  80.7 7.4 %fusion.78 = f32[512,768]{1,0:T(8,128)} fusion(bf16[3072,768]{0,1:T(8,128)(2,1)} %all-gather.5.cloned.1.call-done, f32[3072]{0:T(1024)S(1)} %get-tuple-element.54, f32[512]{0:T(512)S(1)} %copy-done.31, f32[512]{0:T(512)S(1)} %broadcast_multiply_fusion.2, bf16[512,6144]{1,0:T(8,128)(2,1)} %param.10, s32[]{:T(128)S(6)} %select_n.486), kind=kOutput, calls=%fused_computation.211 | convolution fusion | flops 2423783424 | bytes 9453572 | tf_op jit(solution)/shard_map/dot_general | solution.py:32
  88.1 2.9 reshape.277
  91.0 4.5 constant_dynamic-slice_fusion.6
  102.6 3.2 collective-permute-start.6
  105.8 15.3 %all-gather.7.cloned.1.call-done = bf16[3072,768]{1,0:T(8,128)(2,1)} async-done(((bf16[768,768]{1,0:T(8,128)(2,1)}), bf16[3072,768]{1,0:T(8,128)(2,1)}) %all-gather.7.cloned.1.call-update) | async-done | bytes 4718608 | tf_op jit(solution)/shard_map/all_gather | solution.py:78
  121.1 7.0 %convolution_convert_fusion = bf16[512,768]{1,0:T(8,128)(2,1)} fusion(bf16[3072,768]{1,0:T(8,128)(2,1)} %all-gather.7.cloned.1.call-done, bf16[512,3072]{1,0:T(8,128)(2,1)} %get-tuple-element.43, bf16[512,3072]{1,0:T(8,128)(2,1)} %constant_dynamic-update-slice_fusion.7, pred[]{:T(512)S(6)} %eq.6), kind=kOutput, calls=%fused_computation.76 | convolution fusion | flops 2417885184 | bytes 11796481 | tf_op jit(solution)/shard_map/dot_general | solution.py:32
  130.9 3.0 copy.54
  133.9 3.0 copy.55
  139.6 6.0 %fusion.77 = f32[512,768]{1,0:T(8,128)S(1)} fusion(bf16[3072,768]{1,0:T(8,128)(2,1)} %all-gather.7.cloned.1.call-done, f32[3072]{0:T(1024)S(1)} %get-tuple-element.54, f32[512]{0:T(512)S(1)} %copy-done.32, f32[512]{0:T(512)S(1)} %broadcast_multiply_fusion.2, bf16[512,6144]{1,0:T(8,128)(2,1)} %param.10, s32[]{:T(128)S(6)} %select_n.486), kind=kOutput, calls=%fused_computation.210 | convolution fusion | flops 2423783424 | bytes 9453572 | tf_op jit(solution)/shard_map/dot_general | solution.py:32
  149.4 7.7 %collective-permute-done.16 = bf16[512,768]{1,0:T(8,128)(2,1)S(1)} collective-permute-done((bf16[512,768]{1,0:T(8,128)(2,1)}, bf16[512,768]{1,0:T(8,128)(2,1)S(1)}, u32[]{:S(2)}, u32[]{:S(2)}) %collective-permute-start.16) | collective-permute-done | bytes 786464 | tf_op jit(solution)/shard_map/ppermute | solution.py:19
  157.0 4.3 fusion.6
  164.2 2.9 collective-permute-start.10
  167.1 18.8 %collective-permute-done.9 = bf16[512,256]{0,1:T(8,128)(2,1)S(1)} collective-permute-done((bf16[512,256]{0,1:T(8,128)(2,1)S(1)}, bf16[512,256]{0,1:T(8,128)(2,1)S(1)}, u32[]{:S(2)}, u32[]{:S(2)}) %collective-permute-start.9) | collective-permute-done | bytes 262176 | tf_op jit(solution)/shard_map/ppermute | solution.py:24
  186.0 8.3 %multiply_reduce_fusion = (f32[1024]{0:T(1024)S(1)}, f32[1024,4096]{1,0:T(8,128)}) fusion(bf16[4096,256]{0,1:T(8,128)(2,1)S(1)} %constant_dynamic-update-slice_fusion.12, f32[1024,384]{0,1:T(8,128)S(1)} %maximum_add_fusion, f32[128]{0:T(128)S(1)} %copy-done.28, f32[1024]{0:T(1024)S(1)} %add_rsqrt_fusion.1, f32[1024]{0:T(1024)S(1)} %broadcast_multiply_fusion.1), kind=kOutput, calls=%fused_computation.2 | convolution fusion | flops 1082653696 | bytes 18362880 | tf_op jit(solution)/shard_map/qd,kd->qk/dot_general | solution.py:126
  194.3 8.6 %fusion = f32[1024]{0:T(1024)S(1)} fusion(f32[1024,4096]{1,0:T(8,128)} %get-tuple-element.58, f32[1024]{0:T(1024)S(1)} %get-tuple-element.57), kind=kLoop, calls=%fused_computation.5 | loop fusion | flops 12581888 | bytes 16785408 | tf_op jit(solution)/shard_map/reduce_sum | solution.py:127
  202.9 8.2 %fusion.50 = bf16[1024,128]{0,1:T(8,128)(2,1)S(1)} fusion(f32[1024,4096]{1,0:T(8,128)} %get-tuple-element.58, f32[1024]{0:T(1024)S(1)} %fusion, f32[1024]{0:T(1024)S(1)} %get-tuple-element.57, bf16[4096,256]{0,1:T(8,128)(2,1)} %copy-done.23), kind=kOutput, calls=%fused_computation.82 | convolution fusion | flops 1090650112 | bytes 18096128 | tf_op jit(solution)/shard_map/dot_general | solution.py:32
  239.2 2.9 collective-permute-start.15
  246.7 3.0 fusion.81
  249.7 4.3 fusion.83
  258.4 4.1 add_convert_fusion
  262.5 3.4 collective-permute-start.28
  265.9 3.1 fusion.80
  270.7 4.3 fusion.82
  292.8 4.2 all-to-all-start
  311.9 6.4 %collective-permute-done.22 = bf16[4,64,768]{2,1,0:T(8,128)(2,1)S(1)} collective-permute-done((bf16[4,64,768]{2,1,0:T(8,128)(2,1)}, bf16[4,64,768]{2,1,0:T(8,128)(2,1)S(1)}, u32[]{:S(2)}, u32[]{:S(2)}) %collective-permute-start.22) | collective-permute-done | bytes 393248 | tf_op jit(solution)/shard_map/ppermute | solution.py:19
  324.4 4.5 collective-permute-done.33
  332.0 3.7 collective-permute-start.35
  339.4 9.1 %collective-permute-start.36 = (bf16[256,768]{1,0:T(8,128)(2,1)S(1)}, bf16[256,768]{1,0:T(8,128)(2,1)}, u32[]{:S(2)}, u32[]{:S(2)}) collective-permute-start(bf16[256,768]{1,0:T(8,128)(2,1)S(1)} %fusion.60), channel_id=1, source_target_pairs={{0,8},{8,0},{1,9},{9,1},{2,10},{10,2},{3,11},{11,3},{4,12},{12,4},... | collective-permute-start | bytes 1179656 | tf_op jit(solution)/shard_map/ppermute | solution.py:19
  348.5 9.3 %collective-permute-done.36 = bf16[256,768]{1,0:T(8,128)(2,1)} collective-permute-done((bf16[256,768]{1,0:T(8,128)(2,1)S(1)}, bf16[256,768]{1,0:T(8,128)(2,1)}, u32[]{:S(2)}, u32[]{:S(2)}) %collective-permute-start.36) | collective-permute-done | bytes 393248 | tf_op jit(solution)/shard_map/ppermute | solution.py:19
  360.0 9.0 %collective-permute-start.40 = (bf16[512,768]{1,0:T(8,128)(2,1)}, bf16[512,768]{1,0:T(8,128)(2,1)}, u32[]{:S(2)}, u32[]{:S(2)}) collective-permute-start(bf16[512,768]{1,0:T(8,128)(2,1)} %maximum_select_fusion.24), channel_id=1, source_target_pairs={{0,2},{2,4},{4,6},{6,0},{1,3},{3,5},{5,7},{7,1},{8,10},{10,12},{12... | collective-permute-start | bytes 2359304 | tf_op jit(solution)/shard_map/ppermute | solution.py:24
  369.0 6.8 %collective-permute-start.38 = (bf16[512,768]{1,0:T(8,128)(2,1)}, bf16[512,768]{1,0:T(8,128)(2,1)}, u32[]{:S(2)}, u32[]{:S(2)}) collective-permute-start(bf16[512,768]{1,0:T(8,128)(2,1)} %maximum_select_fusion.24), channel_id=1, source_target_pairs={{0,6},{2,0},{4,2},{6,4},{1,7},{3,1},{5,3},{7,5},{8,14},{10,8},{12,... | collective-permute-start | bytes 2359304 | tf_op jit(solution)/shard_map/ppermute | solution.py:24
  375.9 15.3 %collective-permute-done.40 = bf16[512,768]{1,0:T(8,128)(2,1)} collective-permute-done((bf16[512,768]{1,0:T(8,128)(2,1)}, bf16[512,768]{1,0:T(8,128)(2,1)}, u32[]{:S(2)}, u32[]{:S(2)}) %collective-permute-start.40) | collective-permute-done | bytes 786464 | tf_op jit(solution)/shard_map/ppermute | solution.py:24
  396.1 4.0 collective-permute-start.37
  402.4 4.3 collective-permute-start.43
  407.1 11.5 %all-gather.9.cloned.1.call-done = bf16[4096,384]{1,0:T(8,128)(2,1)} async-done(((bf16[512,384]{1,0:T(8,128)(2,1)}), bf16[4096,384]{1,0:T(8,128)(2,1)}) %all-gather.9.cloned.1.call-update) | async-done | bytes 3145744 | tf_op jit(solution)/shard_map/all_gather | solution.py:176
  418.6 3.0 fusion.45
  421.7 2.9 fusion.43
  427.4 3.9 fusion.49
  431.4 23.2 %all-gather.11.cloned.1.call-done = bf16[128,32,384]{2,1,0:T(8,128)(2,1)} async-done(((bf16[8,32,384]{2,1,0:T(8,128)(2,1)}), bf16[128,32,384]{2,1,0:T(8,128)(2,1)}) %all-gather.11.cloned.1.call-update) | async-done | bytes 3145744 | tf_op jit(solution)/shard_map/all_gather | solution.py:188
  454.6 5.5 %convolution_multiply_fusion = f32[384,384]{1,0:T(8,128)} fusion(bf16[4096,384]{1,0:T(8,128)(2,1)} %all-gather.9.cloned.1.call-done, bf16[4096,384]{1,0:T(8,128)(2,1)} %bitcast.149), kind=kOutput, calls=%fused_computation.81 | convolution fusion | flops 1208107008 | bytes 6881280 | tf_op jit(solution)/shard_map/ti,tj->ij/dot_general | solution.py:190
  (263 shorter events, 148.0 us)
Async XLA Ops:
  7.2 63.4 %all-gather.5.cloned.1.call-start = ((), (), s32[]{:S(2)}) async-start(), calls=%async_computation.1 | async-start | bytes 5898240 | tf_op jit(solution)/shard_map/all_gather | solution.py:77
  9.8 111.4 %all-gather.7.cloned.1.call-start = ((), (), s32[]{:S(2)}) async-start(), calls=%async_computation.2 | async-start | bytes 5898240 | tf_op jit(solution)/shard_map/all_gather | solution.py:78
  17.6 12.1 %collective-permute-start = (bf16[64,3072]{1,0:T(8,128)(2,1)S(1)}, bf16[64,3072]{1,0:T(8,128)(2,1)}, u32[]{:S(2)}, u32[]{:S(2)}) collective-permute-start(bf16[64,3072]{1,0:T(8,128)(2,1)S(1)} %multiply_convert_fusion.1), channel_id=1, source_target_pairs={{0,64},{64,0},{1,65},{65,1},{2,66},{66,2},{3,67},{67,3},{4,68},{68... | collective-permute-start | bytes 1179656 | tf_op jit(solution)/shard_map/ppermute | solution.py:19
  29.7 11.2 %collective-permute-start.2 = (bf16[64,3072]{1,0:T(8,128)(2,1)}, bf16[64,3072]{1,0:T(8,128)(2,1)S(1)}, u32[]{:S(2)}, u32[]{:S(2)}) collective-permute-start(bf16[64,3072]{1,0:T(8,128)(2,1)} %collective-permute-done), channel_id=1, source_target_pairs={{0,2},{2,4},{4,6},{6,0},{1,3},{3,5},{5,7},{7,1},{8,10},{10,12},{12... | collective-permute-start | bytes 1179656 | tf_op jit(solution)/shard_map/ppermute | solution.py:24
  31.4 10.3 %collective-permute-start.1 = (bf16[64,3072]{1,0:T(8,128)(2,1)}, bf16[64,3072]{1,0:T(8,128)(2,1)}, u32[]{:S(2)}, u32[]{:S(2)}) collective-permute-start(bf16[64,3072]{1,0:T(8,128)(2,1)} %collective-permute-done), channel_id=1, source_target_pairs={{0,6},{2,0},{4,2},{6,4},{1,7},{3,1},{5,3},{7,5},{8,14},{10,8},{12,... | collective-permute-start | bytes 1179656 | tf_op jit(solution)/shard_map/ppermute | solution.py:24
  41.6 6.3 %collective-permute-start.3 = (bf16[32,3072]{1,0:T(8,128)(2,1)}, bf16[32,3072]{1,0:T(8,128)(2,1)}, u32[]{:S(2)}, u32[]{:S(2)}) collective-permute-start(bf16[32,3072]{1,0:T(8,128)(2,1)} %slice.118), channel_id=1, source_target_pairs={{0,2},{2,4},{4,6},{6,0},{1,3},{3,5},{5,7},{7,1},{8,10},{10,12},{12... | collective-permute-start | bytes 589832 | tf_op jit(solution)/shard_map/ppermute | solution.py:24
  42.6 6.3 %collective-permute-start.4 = (bf16[32,3072]{1,0:T(8,128)(2,1)S(1)}, bf16[32,3072]{1,0:T(8,128)(2,1)S(1)}, u32[]{:S(2)}, u32[]{:S(2)}) collective-permute-start(bf16[32,3072]{1,0:T(8,128)(2,1)S(1)} %slice.119), channel_id=1, source_target_pairs={{0,6},{2,0},{4,2},{6,4},{1,7},{3,1},{5,3},{7,5},{8,14},{10,8},{12,... | collective-permute-start | bytes 589832 | tf_op jit(solution)/shard_map/ppermute | solution.py:24
  57.3 6.6 %collective-permute-start.5 = (bf16[256,3072]{1,0:T(8,128)(2,1)}, bf16[256,3072]{1,0:T(8,128)(2,1)}, u32[]{:S(2)}, u32[]{:S(2)}) collective-permute-start(bf16[256,3072]{1,0:T(8,128)(2,1)} %pad_maximum_fusion.1), channel_id=1, source_target_pairs={{0,1},{1,0},{2,3},{3,2},{4,5},{5,4},{6,7},{7,6},{8,9},{9,8},{10,11... | collective-permute-start | bytes 4718600 | tf_op jit(solution)/shard_map/ppermute | solution.py:19
  102.6 43.0 %collective-permute-start.6 = (bf16[1024,384]{0,1:T(8,128)(2,1)}, bf16[1024,384]{0,1:T(8,128)(2,1)}, u32[]{:S(2)}, u32[]{:S(2)}) collective-permute-start(bf16[1024,384]{0,1:T(8,128)(2,1)} %pad_maximum_fusion.3), channel_id=1, source_target_pairs={{0,64},{64,0},{1,65},{65,1},{2,66},{66,2},{3,67},{67,3},{4,68},{68... | collective-permute-start | bytes 2359304 | tf_op jit(solution)/shard_map/ppermute | solution.py:19
  136.9 20.1 %collective-permute-start.16 = (bf16[512,768]{1,0:T(8,128)(2,1)}, bf16[512,768]{1,0:T(8,128)(2,1)S(1)}, u32[]{:S(2)}, u32[]{:S(2)}) collective-permute-start(bf16[512,768]{1,0:T(8,128)(2,1)} %convolution_convert_fusion), channel_id=1, source_target_pairs={{0,64},{64,0},{1,65},{65,1},{2,66},{66,2},{3,67},{67,3},{4,68},{68... | collective-permute-start | bytes 2359304 | tf_op jit(solution)/shard_map/ppermute | solution.py:19
  147.8 16.3 %collective-permute-start.7 = (bf16[1024,256]{0,1:T(8,128)(2,1)S(1)}, bf16[1024,256]{0,1:T(8,128)(2,1)S(1)}, u32[]{:S(2)}, u32[]{:S(2)}) collective-permute-start(bf16[1024,256]{0,1:T(8,128)(2,1)S(1)} %get-tuple-element.46), channel_id=1, source_target_pairs={{0,48},{16,0},{32,16},{48,32},{1,49},{17,1},{33,17},{49,33},{2,50}... | collective-permute-start | bytes 1572872 | tf_op jit(solution)/shard_map/ppermute | solution.py:24
  148.6 15.4 %collective-permute-start.8 = (bf16[1024,256]{0,1:T(8,128)(2,1)S(1)}, bf16[1024,256]{0,1:T(8,128)(2,1)S(1)}, u32[]{:S(2)}, u32[]{:S(2)}) collective-permute-start(bf16[1024,256]{0,1:T(8,128)(2,1)S(1)} %get-tuple-element.46), channel_id=1, source_target_pairs={{0,16},{16,32},{32,48},{48,0},{1,17},{17,33},{33,49},{49,1},{2,18}... | collective-permute-start | bytes 1572872 | tf_op jit(solution)/shard_map/ppermute | solution.py:24
  161.3 55.3 %collective-permute-start.18 = (bf16[512,768]{1,0:T(8,128)(2,1)}, bf16[512,768]{1,0:T(8,128)(2,1)}, u32[]{:S(2)}, u32[]{:S(2)}) collective-permute-start(bf16[512,768]{1,0:T(8,128)(2,1)} %fusion.6), channel_id=1, source_target_pairs={{0,16},{16,32},{32,48},{48,0},{1,17},{17,33},{33,49},{49,1},{2,18}... | collective-permute-start | bytes 2359304 | tf_op jit(solution)/shard_map/ppermute | solution.py:24
  161.9 56.6 %collective-permute-start.17 = (bf16[512,768]{1,0:T(8,128)(2,1)}, bf16[512,768]{1,0:T(8,128)(2,1)}, u32[]{:S(2)}, u32[]{:S(2)}) collective-permute-start(bf16[512,768]{1,0:T(8,128)(2,1)} %fusion.6), channel_id=1, source_target_pairs={{0,48},{16,0},{32,16},{48,32},{1,49},{17,1},{33,17},{49,33},{2,50}... | collective-permute-start | bytes 2359304 | tf_op jit(solution)/shard_map/ppermute | solution.py:24
  164.0 21.8 %collective-permute-start.9 = (bf16[512,256]{0,1:T(8,128)(2,1)S(1)}, bf16[512,256]{0,1:T(8,128)(2,1)S(1)}, u32[]{:S(2)}, u32[]{:S(2)}) collective-permute-start(bf16[512,256]{0,1:T(8,128)(2,1)S(1)} %slice.123), channel_id=1, source_target_pairs={{0,16},{16,32},{32,48},{48,0},{1,17},{17,33},{33,49},{49,1},{2,18}... | collective-permute-start | bytes 786440 | tf_op jit(solution)/shard_map/ppermute | solution.py:24
  164.2 21.7 %collective-permute-start.10 = (bf16[512,256]{0,1:T(8,128)(2,1)S(1)}, bf16[512,256]{0,1:T(8,128)(2,1)S(1)}, u32[]{:S(2)}, u32[]{:S(2)}) collective-permute-start(bf16[512,256]{0,1:T(8,128)(2,1)S(1)} %slice.124), channel_id=1, source_target_pairs={{0,48},{16,0},{32,16},{48,32},{1,49},{17,1},{33,17},{49,33},{2,50}... | collective-permute-start | bytes 786440 | tf_op jit(solution)/shard_map/ppermute | solution.py:24
  211.9 11.0 %collective-permute-start.11 = (bf16[512,128]{0,1:T(8,128)(2,1)}, bf16[512,128]{0,1:T(8,128)(2,1)}, u32[]{:S(2)}, u32[]{:S(2)}) collective-permute-start(bf16[512,128]{0,1:T(8,128)(2,1)} %get-tuple-element.51), channel_id=1, source_target_pairs={{0,64},{64,0},{1,65},{65,1},{2,66},{66,2},{3,67},{67,3},{4,68},{68... | collective-permute-start | bytes 393224 | tf_op jit(solution)/shard_map/ppermute | solution.py:19
  216.4 33.4 %collective-permute-start.27 = (bf16[768,768]{1,0:T(8,128)(2,1)}, bf16[768,768]{1,0:T(8,128)(2,1)}, u32[]{:S(2)}, u32[]{:S(2)}) collective-permute-start(bf16[768,768]{1,0:T(8,128)(2,1)} %param.17), channel_id=1, source_target_pairs={{0,64},{64,0},{1,65},{65,1},{2,66},{66,2},{3,67},{67,3},{4,68},{68... | collective-permute-start | bytes 3538952 | tf_op jit(solution)/shard_map/ppermute | solution.py:19
  218.4 20.8 %collective-permute-start.19 = (bf16[256,768]{1,0:T(8,128)(2,1)}, bf16[256,768]{1,0:T(8,128)(2,1)}, u32[]{:S(2)}, u32[]{:S(2)}) collective-permute-start(bf16[256,768]{1,0:T(8,128)(2,1)} %slice.131), channel_id=1, source_target_pairs={{0,16},{16,32},{32,48},{48,0},{1,17},{17,33},{33,49},{49,1},{2,18}... | collective-permute-start | bytes 1179656 | tf_op jit(solution)/shard_map/ppermute | solution.py:24
  220.3 21.9 %collective-permute-start.20 = (bf16[256,768]{1,0:T(8,128)(2,1)}, bf16[256,768]{1,0:T(8,128)(2,1)}, u32[]{:S(2)}, u32[]{:S(2)}) collective-permute-start(bf16[256,768]{1,0:T(8,128)(2,1)} %slice.132), channel_id=1, source_target_pairs={{0,48},{16,0},{32,16},{48,32},{1,49},{17,1},{33,17},{49,33},{2,50}... | collective-permute-start | bytes 1179656 | tf_op jit(solution)/shard_map/ppermute | solution.py:24
  224.7 9.9 %collective-permute-start.13 = (bf16[512,256]{0,1:T(8,128)(2,1)}, bf16[512,256]{0,1:T(8,128)(2,1)}, u32[]{:S(2)}, u32[]{:S(2)}) collective-permute-start(bf16[512,256]{0,1:T(8,128)(2,1)} %maximum_select_fusion.27), channel_id=1, source_target_pairs={{0,16},{16,32},{32,48},{48,0},{1,17},{17,33},{33,49},{49,1},{2,18}... | collective-permute-start | bytes 786440 | tf_op jit(solution)/shard_map/ppermute | solution.py:24
  224.7 13.5 %collective-permute-start.12 = (bf16[512,256]{0,1:T(8,128)(2,1)}, bf16[512,256]{0,1:T(8,128)(2,1)}, u32[]{:S(2)}, u32[]{:S(2)}) collective-permute-start(bf16[512,256]{0,1:T(8,128)(2,1)} %maximum_select_fusion.27), channel_id=1, source_target_pairs={{0,48},{16,0},{32,16},{48,32},{1,49},{17,1},{33,17},{49,33},{2,50}... | collective-permute-start | bytes 786440 | tf_op jit(solution)/shard_map/ppermute | solution.py:24
  234.6 23.8 %collective-permute-start.26 = (bf16[256,768]{1,0:T(8,128)(2,1)S(1)}, bf16[256,768]{1,0:T(8,128)(2,1)}, u32[]{:S(2)}, u32[]{:S(2)}) collective-permute-start(bf16[256,768]{1,0:T(8,128)(2,1)S(1)} %copy-done.20), channel_id=1, source_target_pairs={{0,64},{64,0},{1,65},{65,1},{2,66},{66,2},{3,67},{67,3},{4,68},{68... | collective-permute-start | bytes 1179656 | tf_op jit(solution)/shard_map/ppermute | solution.py:19
  238.2 15.9 %collective-permute-start.14 = (bf16[256,256]{0,1:T(8,128)(2,1)S(1)}, bf16[256,256]{0,1:T(8,128)(2,1)S(1)}, u32[]{:S(2)}, u32[]{:S(2)}) collective-permute-start(bf16[256,256]{0,1:T(8,128)(2,1)S(1)} %slice.129), channel_id=1, source_target_pairs={{0,16},{16,32},{32,48},{48,0},{1,17},{17,33},{33,49},{49,1},{2,18}... | collective-permute-start | bytes 393224 | tf_op jit(solution)/shard_map/ppermute | solution.py:24
  239.2 14.9 %collective-permute-start.15 = (bf16[256,256]{0,1:T(8,128)(2,1)S(1)}, bf16[256,256]{0,1:T(8,128)(2,1)S(1)}, u32[]{:S(2)}, u32[]{:S(2)}) collective-permute-start(bf16[256,256]{0,1:T(8,128)(2,1)S(1)} %slice.130), channel_id=1, source_target_pairs={{0,48},{16,0},{32,16},{48,32},{1,49},{17,1},{33,17},{49,33},{2,50}... | collective-permute-start | bytes 393224 | tf_op jit(solution)/shard_map/ppermute | solution.py:24
  262.5 19.3 %collective-permute-start.28 = (bf16[4,256,768]{2,1,0:T(8,128)(2,1)}, bf16[4,256,768]{2,1,0:T(8,128)(2,1)}, u32[]{:S(2)}, u32[]{:S(2)}) collective-permute-start(bf16[4,256,768]{2,1,0:T(8,128)(2,1)} %bitcast.29), channel_id=1, source_target_pairs={{0,1},{1,0},{2,3},{3,2},{4,5},{5,4},{6,7},{7,6},{8,9},{9,8},{10,11... | collective-permute-start | bytes 4718600 | tf_op jit(solution)/shard_map/ppermute | solution.py:19
  270.7 16.5 %collective-permute-start.21 = (bf16[4,256,768]{2,1,0:T(8,128)(2,1)}, bf16[4,256,768]{2,1,0:T(8,128)(2,1)}, u32[]{:S(2)}, u32[]{:S(2)}) collective-permute-start(bf16[4,256,768]{2,1,0:T(8,128)(2,1)} %bitcast.23), channel_id=1, source_target_pairs={{0,1},{1,0},{2,3},{3,2},{4,5},{5,4},{6,7},{7,6},{8,9},{9,8},{10,11... | collective-permute-start | bytes 4718600 | tf_op jit(solution)/shard_map/ppermute | solution.py:19
  284.7 13.0 %collective-permute-start.30 = (bf16[4,64,768]{2,1,0:T(8,128)(2,1)}, bf16[4,64,768]{2,1,0:T(8,128)(2,1)S(1)}, u32[]{:S(2)}, u32[]{:S(2)}) collective-permute-start(bf16[4,64,768]{2,1,0:T(8,128)(2,1)} %get-tuple-element.39), channel_id=1, source_target_pairs={{0,6},{2,4},{4,2},{6,0},{1,7},{3,5},{5,3},{7,1},{8,14},{10,12},{12... | collective-permute-start | bytes 1179656 | tf_op jit(solution)/shard_map/ppermute | solution.py:19
  291.6 10.2 %collective-permute-start.23 = (bf16[4,64,768]{2,1,0:T(8,128)(2,1)}, bf16[4,64,768]{2,1,0:T(8,128)(2,1)}, u32[]{:S(2)}, u32[]{:S(2)}) collective-permute-start(bf16[4,64,768]{2,1,0:T(8,128)(2,1)} %get-tuple-element.37), channel_id=1, source_target_pairs={{0,2},{2,0},{4,6},{6,4},{1,3},{3,1},{5,7},{7,5},{8,10},{10,8},{12,... | collective-permute-start | bytes 1179656 | tf_op jit(solution)/shard_map/ppermute | solution.py:19
  292.8 14.2 %all-to-all-start = ((bf16[8,32,1152]{2,1,0:T(8,128)(2,1)}), bf16[8,32,1152]{2,1,0:T(8,128)(2,1)}, u32[]{:S(2)}, u32[]{:S(2)}) async-start(bf16[8,32,1152]{2,1,0:T(8,128)(2,1)} %copy.52), calls=%async_computation | async-start | bytes 1179648 | tf_op jit(solution)/shard_map/all_to_all | solution.py:84
  297.0 121.6 %all-gather.9.cloned.1.call-start = ((), (), s32[]{:S(2)}) async-start(), calls=%async_computation.3 | async-start | bytes 3538944 | tf_op jit(solution)/shard_map/all_gather | solution.py:176
  297.1 11.5 %collective-permute-start.29 = (bf16[4,64,768]{2,1,0:T(8,128)(2,1)}, bf16[4,64,768]{2,1,0:T(8,128)(2,1)}, u32[]{:S(2)}, u32[]{:S(2)}) collective-permute-start(bf16[4,64,768]{2,1,0:T(8,128)(2,1)} %get-tuple-element.38), channel_id=1, source_target_pairs={{0,6},{2,4},{4,2},{6,0},{1,7},{3,5},{5,3},{7,1},{8,14},{10,12},{12... | collective-permute-start | bytes 1179656 | tf_op jit(solution)/shard_map/ppermute | solution.py:19
  299.6 10.4 %collective-permute-start.31 = (bf16[4,64,768]{2,1,0:T(8,128)(2,1)}, bf16[4,64,768]{2,1,0:T(8,128)(2,1)}, u32[]{:S(2)}, u32[]{:S(2)}) collective-permute-start(bf16[4,64,768]{2,1,0:T(8,128)(2,1)} %add_convert_fusion.2), channel_id=1, source_target_pairs={{0,2},{2,0},{4,6},{6,4},{1,3},{3,1},{5,7},{7,5},{8,10},{10,8},{12,... | collective-permute-start | bytes 1179656 | tf_op jit(solution)/shard_map/ppermute | solution.py:19
  300.3 18.0 %collective-permute-start.22 = (bf16[4,64,768]{2,1,0:T(8,128)(2,1)}, bf16[4,64,768]{2,1,0:T(8,128)(2,1)S(1)}, u32[]{:S(2)}, u32[]{:S(2)}) collective-permute-start(bf16[4,64,768]{2,1,0:T(8,128)(2,1)} %get-tuple-element.36), channel_id=1, source_target_pairs={{0,2},{2,0},{4,6},{6,4},{1,3},{3,1},{5,7},{7,5},{8,10},{10,8},{12,... | collective-permute-start | bytes 1179656 | tf_op jit(solution)/shard_map/ppermute | solution.py:19
  303.9 14.5 %collective-permute-start.24 = (bf16[4,64,768]{2,1,0:T(8,128)(2,1)}, bf16[4,64,768]{2,1,0:T(8,128)(2,1)}, u32[]{:S(2)}, u32[]{:S(2)}) collective-permute-start(bf16[4,64,768]{2,1,0:T(8,128)(2,1)} %add_convert_fusion.3), channel_id=1, source_target_pairs={{0,6},{2,4},{4,2},{6,0},{1,7},{3,5},{5,3},{7,1},{8,14},{10,12},{12... | collective-permute-start | bytes 1179656 | tf_op jit(solution)/shard_map/ppermute | solution.py:19
  311.5 8.6 %collective-permute-start.32 = (bf16[4,32,768]{2,1,0:T(8,128)(2,1)S(1)}, bf16[4,32,768]{2,1,0:T(8,128)(2,1)S(1)}, u32[]{:S(2)}, u32[]{:S(2)}) collective-permute-start(bf16[4,32,768]{2,1,0:T(8,128)(2,1)S(1)} %dynamic-slice_convert_fusion.4), channel_id=1, source_target_pairs={{0,8},{8,0},{1,9},{9,1},{2,10},{10,2},{3,11},{11,3},{4,12},{12,4},... | collective-permute-start | bytes 589832 | tf_op jit(solution)/shard_map/ppermute | solution.py:19
  320.2 8.7 %collective-permute-start.33 = (bf16[4,32,768]{2,1,0:T(8,128)(2,1)S(1)}, bf16[4,32,768]{2,1,0:T(8,128)(2,1)S(1)}, u32[]{:S(2)}, u32[]{:S(2)}) collective-permute-start(bf16[4,32,768]{2,1,0:T(8,128)(2,1)S(1)} %add_convert_fusion.4), channel_id=1, source_target_pairs={{0,64},{64,0},{1,65},{65,1},{2,66},{66,2},{3,67},{67,3},{4,68},{68... | collective-permute-start | bytes 589832 | tf_op jit(solution)/shard_map/ppermute | solution.py:19
  332.0 4.8 %collective-permute-start.35 = (bf16[256,384]{1,0:T(8,128)(2,1)S(1)}, bf16[256,384]{1,0:T(8,128)(2,1)S(1)}, u32[]{:S(2)}, u32[]{:S(2)}) collective-permute-start(bf16[256,384]{1,0:T(8,128)(2,1)S(1)} %get-tuple-element.49), channel_id=1, source_target_pairs={{0,1},{1,0},{2,3},{3,2},{4,5},{5,4},{6,7},{7,6},{8,9},{9,8},{10,11... | collective-permute-start | bytes 589832 | tf_op jit(solution)/shard_map/ppermute | solution.py:19
  337.7 116.9 %all-gather.11.cloned.1.call-start = ((), (), s32[]{:S(2)}) async-start(), calls=%async_computation.4 | async-start | bytes 3342336 | tf_op jit(solution)/shard_map/all_gather | solution.py:188
  339.4 18.4 %collective-permute-start.36 = (bf16[256,768]{1,0:T(8,128)(2,1)S(1)}, bf16[256,768]{1,0:T(8,128)(2,1)}, u32[]{:S(2)}, u32[]{:S(2)}) collective-permute-start(bf16[256,768]{1,0:T(8,128)(2,1)S(1)} %fusion.60), channel_id=1, source_target_pairs={{0,8},{8,0},{1,9},{9,1},{2,10},{10,2},{3,11},{11,3},{4,12},{12,4},... | collective-permute-start | bytes 1179656 | tf_op jit(solution)/shard_map/ppermute | solution.py:19
  360.0 31.2 %collective-permute-start.40 = (bf16[512,768]{1,0:T(8,128)(2,1)}, bf16[512,768]{1,0:T(8,128)(2,1)}, u32[]{:S(2)}, u32[]{:S(2)}) collective-permute-start(bf16[512,768]{1,0:T(8,128)(2,1)} %maximum_select_fusion.24), channel_id=1, source_target_pairs={{0,2},{2,4},{4,6},{6,0},{1,3},{3,5},{5,7},{7,1},{8,10},{10,12},{12... | collective-permute-start | bytes 2359304 | tf_op jit(solution)/shard_map/ppermute | solution.py:24
  369.0 23.3 %collective-permute-start.38 = (bf16[512,768]{1,0:T(8,128)(2,1)}, bf16[512,768]{1,0:T(8,128)(2,1)}, u32[]{:S(2)}, u32[]{:S(2)}) collective-permute-start(bf16[512,768]{1,0:T(8,128)(2,1)} %maximum_select_fusion.24), channel_id=1, source_target_pairs={{0,6},{2,0},{4,2},{6,4},{1,7},{3,1},{5,3},{7,5},{8,14},{10,8},{12,... | collective-permute-start | bytes 2359304 | tf_op jit(solution)/shard_map/ppermute | solution.py:24
  392.2 8.5 %collective-permute-start.41 = (bf16[256,768]{1,0:T(8,128)(2,1)S(1)}, bf16[256,768]{1,0:T(8,128)(2,1)S(1)}, u32[]{:S(2)}, u32[]{:S(2)}) collective-permute-start(bf16[256,768]{1,0:T(8,128)(2,1)S(1)} %slice.141), channel_id=1, source_target_pairs={{0,2},{2,4},{4,6},{6,0},{1,3},{3,5},{5,7},{7,1},{8,10},{10,12},{12... | collective-permute-start | bytes 1179656 | tf_op jit(solution)/shard_map/ppermute | solution.py:24
  393.4 8.2 %collective-permute-start.42 = (bf16[256,768]{1,0:T(8,128)(2,1)S(1)}, bf16[256,768]{1,0:T(8,128)(2,1)S(1)}, u32[]{:S(2)}, u32[]{:S(2)}) collective-permute-start(bf16[256,768]{1,0:T(8,128)(2,1)S(1)} %slice.142), channel_id=1, source_target_pairs={{0,6},{2,0},{4,2},{6,4},{1,7},{3,1},{5,3},{7,5},{8,14},{10,8},{12,... | collective-permute-start | bytes 1179656 | tf_op jit(solution)/shard_map/ppermute | solution.py:24
  396.1 11.1 %collective-permute-start.37 = (bf16[512,768]{1,0:T(8,128)(2,1)}, bf16[512,768]{1,0:T(8,128)(2,1)}, u32[]{:S(2)}, u32[]{:S(2)}) collective-permute-start(bf16[512,768]{1,0:T(8,128)(2,1)} %maximum_select_fusion.24), channel_id=1, source_target_pairs={{0,1},{1,0},{2,3},{3,2},{4,5},{5,4},{6,7},{7,6},{8,9},{9,8},{10,11... | collective-permute-start | bytes 2359304 | tf_op jit(solution)/shard_map/ppermute | solution.py:19
  402.4 19.3 %collective-permute-start.43 = (bf16[512,768]{1,0:T(8,128)(2,1)}, bf16[512,768]{1,0:T(8,128)(2,1)}, u32[]{:S(2)}, u32[]{:S(2)}) collective-permute-start(bf16[512,768]{1,0:T(8,128)(2,1)} %constant_dynamic-update-slice_fusion.17), channel_id=1, source_target_pairs={{0,1},{1,0},{2,3},{3,2},{4,5},{5,4},{6,7},{7,6},{8,9},{9,8},{10,11... | collective-permute-start | bytes 2359304 | tf_op jit(solution)/shard_map/ppermute | solution.py:19
  406.6 18.0 %collective-permute-start.44 = (bf16[512,768]{1,0:T(8,128)(2,1)}, bf16[512,768]{1,0:T(8,128)(2,1)}, u32[]{:S(2)}, u32[]{:S(2)}) collective-permute-start(bf16[512,768]{1,0:T(8,128)(2,1)} %collective-permute-done.40), channel_id=1, source_target_pairs={{0,1},{1,0},{2,3},{3,2},{4,5},{5,4},{6,7},{7,6},{8,9},{9,8},{10,11... | collective-permute-start | bytes 2359304 | tf_op jit(solution)/shard_map/ppermute | solution.py:19
  406.6 20.8 %collective-permute-start.39 = (bf16[512,768]{1,0:T(8,128)(2,1)}, bf16[512,768]{1,0:T(8,128)(2,1)}, u32[]{:S(2)}, u32[]{:S(2)}) collective-permute-start(bf16[512,768]{1,0:T(8,128)(2,1)} %collective-permute-done.38), channel_id=1, source_target_pairs={{0,1},{1,0},{2,3},{3,2},{4,5},{5,4},{6,7},{7,6},{8,9},{9,8},{10,11... | collective-permute-start | bytes 2359304 | tf_op jit(solution)/shard_map/ppermute | solution.py:19
  (40 other events, 416.4 us)
Sparse Core Ops, SparseCore 0:
  10.2 56.0 all-gather.4
  68.0 53.1 all-gather.6
  337.8 80.7 all-gather.8
  420.2 34.3 all-gather.10
